TPU v7x, 128 devices: a whole 4x4x4 slice. The times are simulated.
128 devices in a mesh: vol: 16 (over x_hi, y, core), rate: 8 (over z, x_lo).
Axes of the slice: x: 4 (x_hi: 2, x_lo: 2; x = x_hi * 2 + x_lo), y: 4, z: 4, core: 2. Of those that a mesh axis runs over, the one named last changes fastest.
Arguments:
- value_next: float32 [256, 64, 2048], P('vol', 'rate'), may hold values from -6 to 6
- risk_cost: float32 [8, 256], P(None, 'vol'), may hold values from -4 to 4
- band_start: int32 [8, 2048], replicated, may hold values from 0 to 2046, as said below
- band_weight: float32 [8, 2048], replicated, may hold values from 0 to 1
- felicity_array: float32 [2048], replicated, may hold values from -4 to 4
Outputs:
- value_now: float32 [256, 64, 2048], P('vol', 'rate')
Inputs may be any that keep to these rules, and one draw needn't show every extreme that they name: band_start[a, w] lies between w - 64 and w + 62 for every allocation a and wealth point w.
All inputs are finite; a program needn't handle non-finite values.
Results may differ from a plain program's by a relative error of at most 0.00002.
Values sent between devices are 32-bit elements; how exact they have to be, the bound alone decides.
No kernel may reach another device: no remote copies, remote signals or barrier semaphores. Data moves between devices by JAX's collectives and lax.ppermute only.
A program may use at most 320 MiB of HBM per device.

v0:
```python
import jax
import jax.numpy as jnp
from jax import lax
from jax.sharding import PartitionSpec as P

SECTIONS = 2


hermite_weights = (
    0.000548269,
    0.030757124,
    0.240123178,
    0.457142857,
    0.240123178,
    0.030757124,
    0.000548269,
)
discount = 0.96
smoothing_coefficient = 0.5


def with_halo(block, sides, width):
    for axis, dim in sides:
        count = lax.axis_size(axis)
        forward = [(i, i + 1) for i in range(count - 1)]
        backward = [(target, source) for source, target in forward]
        low = lax.ppermute(
            lax.slice_in_dim(block, block.shape[dim] - width, None, axis=dim), axis, forward
        )
        high = lax.ppermute(lax.slice_in_dim(block, 0, width, axis=dim), axis, backward)
        block = jnp.concatenate([low, block, high], axis=dim)
    return block


def narrow(padded, along):
    section_length = padded.shape[along] - 6
    result = hermite_weights[0] * lax.slice_in_dim(padded, 0, section_length, axis=along)
    for start_shift in range(1, 7):
        result = result + hermite_weights[start_shift] * lax.slice_in_dim(
            padded, start_shift, start_shift + section_length, axis=along
        )
    return result


def settle(expected, risk_part, band_start, band_weight, felicity_array):
    normalizer_sum = jnp.zeros(expected.shape, jnp.float32)
    for option in range(band_start.shape[0]):
        lower_node = jnp.take(expected, band_start[option], axis=2)
        higher_node = jnp.take(expected, band_start[option] + 1, axis=2)
        right_share = band_weight[option][None, None, :]
        cont = (1.0 - right_share) * lower_node + right_share * higher_node
        candidate_logits = discount * cont - risk_part[option][:, None, None]
        normalizer_sum = normalizer_sum + jnp.exp(candidate_logits / smoothing_coefficient)
    return smoothing_coefficient * jnp.log(normalizer_sum) + felicity_array[None, None, :]


def on_device(value_next, risk_cost, band_start, band_weight, felicity_array):
    ongoing_estimate = value_next
    for age_index in range(SECTIONS):
        vol_padded = with_halo(ongoing_estimate, (("vol", 0),), 3)
        vol_smooth = narrow(vol_padded, 0)
        rate_with_border = with_halo(vol_smooth, (("rate", 1),), 3)
        expected = narrow(rate_with_border, 1)
        ongoing_estimate = settle(expected, risk_cost, band_start, band_weight, felicity_array)
    return ongoing_estimate


def solution(mesh):
    return jax.shard_map(
        on_device,
        mesh=mesh,
        in_specs=(P("vol", "rate", None), P(None, "vol"), P(), P(), P()),
        out_specs=P("vol", "rate", None),
        check_vma=False,
    )
```

profile of v0, /device:TPU:25, one launch (start us, length us, event | category | flops | bytes accessed | tf_op | source)
XLA Modules:
  0.0 904.4 jit_solution(8542926271410951632)
XLA Ops:
  26.9 10.2 %collective-permute-done.3 = f32[16,3,2048]{2,0,1:T(8,128)S(1)} collective-permute-done((f32[16,3,2048]{2,0,1:T(8,128)S(1)}, f32[16,3,2048]{2,0,1:T(8,128)S(1)}, u32[]{:S(2)}, u32[]{:S(2)}) %collective-permute-start.3) | collective-permute-done | bytes 393248 | tf_op jit(solution)/shard_map/ppermute | solution.py:30
  44.0 19.2 %gather_fusion = f32[2048,16,8]{1,2,0:T(8,128)} fusion(f32[16,8,2048]{0,1,2:T(8,128)} %copy.164, s32[2048]{0:T(1024)S(1)} %get-tuple-element.79), kind=kCustom, calls=%fused_computation.clone | custom fusion | bytes 2105344 | tf_op jit(solution)/shard_map/jit(_take)/gather | solution.py:48
  68.6 19.2 %gather_fusion.1 = f32[2048,16,8]{1,2,0:T(8,128)} fusion(f32[16,8,2048]{0,1,2:T(8,128)} %copy.164, s32[2048]{0:T(1024)S(1)} %get-tuple-element.78), kind=kCustom, calls=%fused_computation.1.clone | custom fusion | bytes 2105344 | tf_op jit(solution)/shard_map/jit(_take)/gather | solution.py:49
  93.2 19.2 %gather_fusion.2 = f32[2048,16,8]{1,2,0:T(8,128)} fusion(f32[16,8,2048]{0,1,2:T(8,128)} %copy.164, s32[2048]{0:T(1024)S(1)} %get-tuple-element.50), kind=kCustom, calls=%fused_computation.2.clone | custom fusion | bytes 2105344 | tf_op jit(solution)/shard_map/jit(_take)/gather | solution.py:48
  117.8 19.2 %gather_fusion.3 = f32[2048,16,8]{1,2,0:T(8,128)} fusion(f32[16,8,2048]{0,1,2:T(8,128)} %copy.164, s32[2048]{0:T(1024)S(1)} %get-tuple-element.51), kind=kCustom, calls=%fused_computation.3.clone | custom fusion | bytes 2105344 | tf_op jit(solution)/shard_map/jit(_take)/gather | solution.py:49
  143.2 19.2 %gather_fusion.4 = f32[2048,16,8]{1,2,0:T(8,128)} fusion(f32[16,8,2048]{0,1,2:T(8,128)} %copy.164, s32[2048]{0:T(1024)S(1)} %get-tuple-element.73), kind=kCustom, calls=%fused_computation.4.clone | custom fusion | bytes 2105344 | tf_op jit(solution)/shard_map/jit(_take)/gather | solution.py:48
  168.5 19.2 %gather_fusion.5 = f32[2048,16,8]{1,2,0:T(8,128)} fusion(f32[16,8,2048]{0,1,2:T(8,128)} %copy.164, s32[2048]{0:T(1024)S(1)} %get-tuple-element.72), kind=kCustom, calls=%fused_computation.5.clone | custom fusion | bytes 2105344 | tf_op jit(solution)/shard_map/jit(_take)/gather | solution.py:49
  187.7 6.2 copy.175
  193.9 19.2 %gather_fusion.6 = f32[2048,16,8]{1,2,0:T(8,128)} fusion(f32[16,8,2048]{0,1,2:T(8,128)} %copy.164, s32[2048]{0:T(1024)S(1)} %get-tuple-element.54), kind=kCustom, calls=%fused_computation.6.clone | custom fusion | bytes 2105344 | tf_op jit(solution)/shard_map/jit(_take)/gather | solution.py:48
  219.3 19.2 %gather_fusion.7 = f32[2048,16,8]{1,2,0:T(8,128)} fusion(f32[16,8,2048]{0,1,2:T(8,128)} %copy.164, s32[2048]{0:T(1024)S(1)} %get-tuple-element.55), kind=kCustom, calls=%fused_computation.7.clone | custom fusion | bytes 2105344 | tf_op jit(solution)/shard_map/jit(_take)/gather | solution.py:49
  244.7 19.2 %gather_fusion.8 = f32[2048,16,8]{1,2,0:T(8,128)} fusion(f32[16,8,2048]{0,1,2:T(8,128)} %copy.164, s32[2048]{0:T(1024)S(1)} %get-tuple-element.75), kind=kCustom, calls=%fused_computation.8.clone | custom fusion | bytes 2105344 | tf_op jit(solution)/shard_map/jit(_take)/gather | solution.py:48
  263.9 6.2 copy.181
  270.1 19.2 %gather_fusion.9 = f32[2048,16,8]{1,2,0:T(8,128)} fusion(f32[16,8,2048]{0,1,2:T(8,128)} %copy.164, s32[2048]{0:T(1024)S(1)} %get-tuple-element.74), kind=kCustom, calls=%fused_computation.9.clone | custom fusion | bytes 2105344 | tf_op jit(solution)/shard_map/jit(_take)/gather | solution.py:49
  295.4 19.2 %gather_fusion.10 = f32[2048,16,8]{1,2,0:T(8,128)} fusion(f32[16,8,2048]{0,1,2:T(8,128)} %copy.164, s32[2048]{0:T(1024)S(1)} %get-tuple-element.58), kind=kCustom, calls=%fused_computation.10.clone | custom fusion | bytes 2105344 | tf_op jit(solution)/shard_map/jit(_take)/gather | solution.py:48
  314.6 6.2 copy.185
  320.8 19.2 %gather_fusion.11 = f32[2048,16,8]{1,2,0:T(8,128)} fusion(f32[16,8,2048]{0,1,2:T(8,128)} %copy.164, s32[2048]{0:T(1024)S(1)} %get-tuple-element.59), kind=kCustom, calls=%fused_computation.11.clone | custom fusion | bytes 2105344 | tf_op jit(solution)/shard_map/jit(_take)/gather | solution.py:49
  346.2 19.2 %gather_fusion.12 = f32[2048,16,8]{1,2,0:T(8,128)} fusion(f32[16,8,2048]{0,1,2:T(8,128)} %copy.164, s32[2048]{0:T(1024)S(1)} %get-tuple-element.77), kind=kCustom, calls=%fused_computation.12.clone | custom fusion | bytes 2105344 | tf_op jit(solution)/shard_map/jit(_take)/gather | solution.py:48
  371.5 19.2 %gather_fusion.13 = f32[2048,16,8]{1,2,0:T(8,128)} fusion(f32[16,8,2048]{0,1,2:T(8,128)} %copy.164, s32[2048]{0:T(1024)S(1)} %get-tuple-element.76), kind=kCustom, calls=%fused_computation.13.clone | custom fusion | bytes 2105344 | tf_op jit(solution)/shard_map/jit(_take)/gather | solution.py:49
  390.8 6.7 copy.191
  397.4 19.2 %gather_fusion.14 = f32[2048,16,8]{1,2,0:T(8,128)} fusion(f32[16,8,2048]{0,1,2:T(8,128)} %copy.164, s32[2048]{0:T(1024)S(1)} %get-tuple-element.62), kind=kCustom, calls=%fused_computation.14.clone | custom fusion | bytes 2105344 | tf_op jit(solution)/shard_map/jit(_take)/gather | solution.py:48
  422.8 19.2 %gather_fusion.15 = f32[2048,16,8]{1,2,0:T(8,128)} fusion(f32[16,8,2048]{0,1,2:T(8,128)} %copy.164, s32[2048]{0:T(1024)S(1)} %get-tuple-element.63), kind=kCustom, calls=%fused_computation.15.clone | custom fusion | bytes 2105344 | tf_op jit(solution)/shard_map/jit(_take)/gather | solution.py:49
  448.2 6.8 fusion.112
  462.1 8.0 collective-permute-done.5
  478.2 8.5 collective-permute-done.7
  493.5 19.2 %gather_fusion.16 = f32[2048,16,8]{1,2,0:T(8,128)} fusion(f32[16,8,2048]{0,1,2:T(8,128)} %copy.200, s32[2048]{0:T(1024)S(1)} %get-tuple-element.79), kind=kCustom, calls=%fused_computation.16.clone | custom fusion | bytes 2105344 | tf_op jit(solution)/shard_map/jit(_take)/gather | solution.py:48
  512.6 19.1 %gather_fusion.17 = f32[2048,16,8]{1,2,0:T(8,128)} fusion(f32[16,8,2048]{0,1,2:T(8,128)} %copy.200, s32[2048]{0:T(1024)S(1)} %get-tuple-element.78), kind=kCustom, calls=%fused_computation.17.clone | custom fusion | bytes 2105344 | tf_op jit(solution)/shard_map/jit(_take)/gather | solution.py:49
  531.7 19.1 %gather_fusion.18 = f32[2048,16,8]{1,2,0:T(8,128)} fusion(f32[16,8,2048]{0,1,2:T(8,128)} %copy.200, s32[2048]{0:T(1024)S(1)} %get-tuple-element.50), kind=kCustom, calls=%fused_computation.18.clone | custom fusion | bytes 2105344 | tf_op jit(solution)/shard_map/jit(_take)/gather | solution.py:48
  550.8 19.1 %gather_fusion.19 = f32[2048,16,8]{1,2,0:T(8,128)} fusion(f32[16,8,2048]{0,1,2:T(8,128)} %copy.200, s32[2048]{0:T(1024)S(1)} %get-tuple-element.51), kind=kCustom, calls=%fused_computation.19.clone | custom fusion | bytes 2105344 | tf_op jit(solution)/shard_map/jit(_take)/gather | solution.py:49
  569.9 19.3 %gather_fusion.20 = f32[2048,16,8]{1,2,0:T(8,128)} fusion(f32[16,8,2048]{0,1,2:T(8,128)} %copy.200, s32[2048]{0:T(1024)S(1)} %get-tuple-element.73), kind=kCustom, calls=%fused_computation.20.clone | custom fusion | bytes 2105344 | tf_op jit(solution)/shard_map/jit(_take)/gather | solution.py:48
  589.2 19.2 %gather_fusion.21 = f32[2048,16,8]{1,2,0:T(8,128)} fusion(f32[16,8,2048]{0,1,2:T(8,128)} %copy.200, s32[2048]{0:T(1024)S(1)} %get-tuple-element.72), kind=kCustom, calls=%fused_computation.21.clone | custom fusion | bytes 2105344 | tf_op jit(solution)/shard_map/jit(_take)/gather | solution.py:49
  608.4 19.3 %gather_fusion.22 = f32[2048,16,8]{1,2,0:T(8,128)} fusion(f32[16,8,2048]{0,1,2:T(8,128)} %copy.200, s32[2048]{0:T(1024)S(1)} %get-tuple-element.54), kind=kCustom, calls=%fused_computation.22.clone | custom fusion | bytes 2105344 | tf_op jit(solution)/shard_map/jit(_take)/gather | solution.py:48
  627.6 19.2 %gather_fusion.23 = f32[2048,16,8]{1,2,0:T(8,128)} fusion(f32[16,8,2048]{0,1,2:T(8,128)} %copy.200, s32[2048]{0:T(1024)S(1)} %get-tuple-element.55), kind=kCustom, calls=%fused_computation.23.clone | custom fusion | bytes 2105344 | tf_op jit(solution)/shard_map/jit(_take)/gather | solution.py:49
  646.8 19.1 %gather_fusion.24 = f32[2048,16,8]{1,2,0:T(8,128)} fusion(f32[16,8,2048]{0,1,2:T(8,128)} %copy.200, s32[2048]{0:T(1024)S(1)} %get-tuple-element.75), kind=kCustom, calls=%fused_computation.24.clone | custom fusion | bytes 2105344 | tf_op jit(solution)/shard_map/jit(_take)/gather | solution.py:48
  665.8 19.1 %gather_fusion.25 = f32[2048,16,8]{1,2,0:T(8,128)} fusion(f32[16,8,2048]{0,1,2:T(8,128)} %copy.200, s32[2048]{0:T(1024)S(1)} %get-tuple-element.74), kind=kCustom, calls=%fused_computation.25.clone | custom fusion | bytes 2105344 | tf_op jit(solution)/shard_map/jit(_take)/gather | solution.py:49
  684.9 19.1 %gather_fusion.26 = f32[2048,16,8]{1,2,0:T(8,128)} fusion(f32[16,8,2048]{0,1,2:T(8,128)} %copy.200, s32[2048]{0:T(1024)S(1)} %get-tuple-element.58), kind=kCustom, calls=%fused_computation.26.clone | custom fusion | bytes 2105344 | tf_op jit(solution)/shard_map/jit(_take)/gather | solution.py:48
  704.0 19.1 %gather_fusion.27 = f32[2048,16,8]{1,2,0:T(8,128)} fusion(f32[16,8,2048]{0,1,2:T(8,128)} %copy.200, s32[2048]{0:T(1024)S(1)} %get-tuple-element.59), kind=kCustom, calls=%fused_computation.27.clone | custom fusion | bytes 2105344 | tf_op jit(solution)/shard_map/jit(_take)/gather | solution.py:49
  723.2 19.2 %gather_fusion.28 = f32[2048,16,8]{1,2,0:T(8,128)} fusion(f32[16,8,2048]{0,1,2:T(8,128)} %copy.200, s32[2048]{0:T(1024)S(1)} %get-tuple-element.77), kind=kCustom, calls=%fused_computation.28.clone | custom fusion | bytes 2105344 | tf_op jit(solution)/shard_map/jit(_take)/gather | solution.py:48
  742.4 19.2 %gather_fusion.29 = f32[2048,16,8]{1,2,0:T(8,128)} fusion(f32[16,8,2048]{0,1,2:T(8,128)} %copy.200, s32[2048]{0:T(1024)S(1)} %get-tuple-element.76), kind=kCustom, calls=%fused_computation.29.clone | custom fusion | bytes 2105344 | tf_op jit(solution)/shard_map/jit(_take)/gather | solution.py:49
  761.6 19.2 %gather_fusion.30 = f32[2048,16,8]{1,2,0:T(8,128)} fusion(f32[16,8,2048]{0,1,2:T(8,128)} %copy.200, s32[2048]{0:T(1024)S(1)} %get-tuple-element.62), kind=kCustom, calls=%fused_computation.30.clone | custom fusion | bytes 2105344 | tf_op jit(solution)/shard_map/jit(_take)/gather | solution.py:48
  780.8 19.2 %gather_fusion.31 = f32[2048,16,8]{1,2,0:T(8,128)} fusion(f32[16,8,2048]{0,1,2:T(8,128)} %copy.200, s32[2048]{0:T(1024)S(1)} %get-tuple-element.63), kind=kCustom, calls=%fused_computation.31.clone | custom fusion | bytes 2105344 | tf_op jit(solution)/shard_map/jit(_take)/gather | solution.py:49
  828.5 6.2 copy.211
  834.7 6.2 copy.213
  847.0 6.2 copy.217
  853.2 6.2 copy.219
  859.4 6.2 copy.221
  865.5 6.2 copy.223
  871.7 6.4 copy.225
  896.6 7.6 fusion.62
  (74 shorter events, 180.0 us)
Async XLA Ops:
  1.1 9.8 %collective-permute-start = (f32[3,8,2048]{2,1,0:T(8,128)S(1)}, f32[3,8,2048]{2,1,0:T(8,128)S(1)}, u32[]{:S(2)}, u32[]{:S(2)}) collective-permute-start(f32[3,8,2048]{2,1,0:T(8,128)S(1)} %get-tuple-element.14), channel_id=1, source_target_pairs={{0,8},{8,16},{16,24},{24,32},{32,40},{40,48},{48,56},{56,64},{64,7... | collective-permute-start | bytes 589832 | tf_op jit(solution)/shard_map/ppermute | solution.py:27
  5.9 10.6 %collective-permute-start.1 = (f32[3,8,2048]{2,1,0:T(8,128)S(1)}, f32[3,8,2048]{2,1,0:T(8,128)S(1)}, u32[]{:S(2)}, u32[]{:S(2)}) collective-permute-start(f32[3,8,2048]{2,1,0:T(8,128)S(1)} %get-tuple-element.15), channel_id=1, source_target_pairs={{8,0},{16,8},{24,16},{32,24},{40,32},{48,40},{56,48},{64,56},{72,6... | collective-permute-start | bytes 589832 | tf_op jit(solution)/shard_map/ppermute | solution.py:30
  9.2 13.4 %copy-start.1 = (f32[8,16]{1,0:T(8,128)S(1)}, f32[8,16]{1,0:T(8,128)}, u32[]{:S(2)}) copy-start(f32[8,16]{1,0:T(8,128)} %param.8) | copy-start | bytes 1540
  18.7 7.8 collective-permute-start.2
  21.2 15.8 %collective-permute-start.3 = (f32[16,3,2048]{2,0,1:T(8,128)S(1)}, f32[16,3,2048]{2,0,1:T(8,128)S(1)}, u32[]{:S(2)}, u32[]{:S(2)}) collective-permute-start(f32[16,3,2048]{2,0,1:T(8,128)S(1)} %copy.162), channel_id=1, source_target_pairs={{1,0},{2,1},{3,2},{4,3},{5,4},{6,5},{7,6},{9,8},{10,9},{11,10},{12... | collective-permute-start | bytes 1179656 | tf_op jit(solution)/shard_map/ppermute | solution.py:30
  416.7 31.5 %copy-start = (f32[2048]{0:T(1024)S(1)}, f32[2048]{0:T(1024)}, u32[]{:S(2)}) copy-start(f32[2048]{0:T(1024)} %param.11) | copy-start | bytes 24580
  455.0 7.1 collective-permute-start.4
  459.5 10.6 %collective-permute-start.5 = (f32[3,8,2048]{2,1,0:T(8,128)S(1)}, f32[3,8,2048]{2,1,0:T(8,128)S(1)}, u32[]{:S(2)}, u32[]{:S(2)}) collective-permute-start(f32[3,8,2048]{2,1,0:T(8,128)S(1)} %get-tuple-element.9), channel_id=1, source_target_pairs={{8,0},{16,8},{24,16},{32,24},{40,32},{48,40},{56,48},{64,56},{72,6... | collective-permute-start | bytes 589832 | tf_op jit(solution)/shard_map/ppermute | solution.py:30
  471.0 6.9 collective-permute-start.6
  473.5 13.2 %collective-permute-start.7 = (f32[16,3,2048]{2,0,1:T(8,128)S(1)}, f32[16,3,2048]{2,0,1:T(8,128)S(1)}, u32[]{:S(2)}, u32[]{:S(2)}) collective-permute-start(f32[16,3,2048]{2,0,1:T(8,128)S(1)} %copy.198), channel_id=1, source_target_pairs={{1,0},{2,1},{3,2},{4,3},{5,4},{6,5},{7,6},{9,8},{10,9},{11,10},{12... | collective-permute-start | bytes 1179656 | tf_op jit(solution)/shard_map/ppermute | solution.py:30
where the time goes:
time: 913 us; the launch traced here: 904 us
  local copies, waits for them, and re-layouts  825 us (90%)
  waiting for transfers between devices  38.7 us (4%)
  starting transfers between devices  20.3 us (2%)
  other arithmetic  19.6 us (2%)
    gather x32, local copies, waits for them, and re-layouts, settle(): higher_node = jnp.take(expected, band_start[option] + 1, axis=2)  404 us
    gather x32, local copies, waits for them, and re-layouts, settle(): lower_node = jnp.take(expected, band_start[option], axis=2)  403 us
    ppermute x4, waiting for transfers between devices, with_halo(): lax.ppermute(lax.slice_in_dim(block, 0, width, axis=dim), axis, backward)  30.8 us
  transfers between devices with their start and end apart: 8, of which 7 were waited for; matrix products, arithmetic and copies ran while one was open for 1% of the time, Pallas kernels for 0%

commit v1 on v0

v1 whole, which is shorter than its diff:
```python
import functools

import jax
import jax.numpy as jnp
from jax import lax
from jax.experimental import pallas as pl
from jax.experimental.pallas import tpu as pltpu
from jax.sharding import PartitionSpec as P

GAUSS = (
    0.000548269,
    0.030757124,
    0.240123178,
    0.457142857,
    0.240123178,
    0.030757124,
    0.000548269,
)
REACH = 3
WIDE = 2 * REACH
LOG2E = 1.4426950408889634
LN2 = 0.6931471805599453
DISCOUNT = 0.96
SMOOTHING = 0.5
LANES = 128
SCALE = DISCOUNT / SMOOTHING * LOG2E

F32 = jnp.float32
BF16 = jnp.bfloat16

CHUNKS = 4
EDGE = 8
SMOOTH_COST = 10**9
SETTLE_COST = 4 * 10**9

SMEM = pl.BlockSpec(memory_space=pltpu.SMEM)
VMEM = pl.BlockSpec(memory_space=pltpu.VMEM)
VMEM_LIMIT = 24 * 2**20


def repeat(count, step, body):
    turns = count // step
    if turns > 1:

        def turn(t, carry):
            for q in range(step):
                body(t * step + q)
            return carry

        lax.fori_loop(0, turns, turn, 0)
        done = turns * step
    else:
        done = 0
    for q in range(done, count):
        body(q)


def lanes_of(tile, count=1):
    if isinstance(tile, int):
        return pl.ds(tile * LANES, count * LANES)
    return pl.ds(pl.multiple_of(tile * LANES, LANES), count * LANES)


def cost(flops):
    return pl.CostEstimate(flops=flops, bytes_accessed=0, transcendentals=0)


def smooth_rows(layers):
    rows = []
    for i in range(len(layers) - WIDE):
        total = GAUSS[REACH] * layers[i + REACH]
        for j in range(REACH):
            total = total + GAUSS[j] * (layers[i + j] + layers[i + WIDE - j])
        rows.append(total)
    return rows


def inner_kernel(own, sent, kept):
    def body(tile):
        at = lanes_of(tile)
        first = EDGE // 2
        layers = [own[i, :, at] for i in range(first - REACH, own.shape[0] - first + REACH)]
        turned = jnp.swapaxes(jnp.stack(smooth_rows(layers)), 0, 1)
        sent[:, :, at] = turned[:WIDE]
        kept[:, :, at] = turned[WIDE:]

    repeat(own.shape[-1] // LANES, 2, body)


def outer_kernel(side, own, near, far, sent, kept):
    first_core = side[0] != 0

    def body(tile):
        at = lanes_of(tile)
        pairs = [(near[i, :, at], far[i, :, at]) for i in range(WIDE)]
        low = [jnp.where(first_core, f, n) for n, f in pairs]
        high = [jnp.where(first_core, n, f) for n, f in pairs]
        count = own.shape[0]
        half = EDGE // 2
        low += [own[i, :, at] for i in range(half + REACH)]
        high = [own[i, :, at] for i in range(count - half - REACH, count)] + high
        nothing = jnp.zeros_like(low[0])
        rows = [nothing] + smooth_rows(low) + smooth_rows(high) + [nothing]
        turned = jnp.swapaxes(jnp.stack(rows), 0, 1)
        sent[:, :, at] = turned[:WIDE]
        kept[:, :, at] = turned[WIDE:]

    repeat(own.shape[-1] // LANES, 2, body)


def block(array_or_shape, width, index):
    shape = getattr(array_or_shape, "shape", array_or_shape)
    return pl.BlockSpec((*shape[:2], width), lambda i: (0, 0, i if index is None else index))


def smooth_inner(own):
    vols, rates, width = own.shape
    outs = [jax.ShapeDtypeStruct((n, vols - EDGE, width), F32) for n in (WIDE, rates - WIDE)]
    wide = width // CHUNKS
    return pl.pallas_call(
        inner_kernel,
        grid=(CHUNKS,),
        out_shape=outs,
        in_specs=[block(own, wide, None)],
        out_specs=[block(o, wide, None) for o in outs],
        compiler_params=pltpu.CompilerParams(vmem_limit_bytes=VMEM_LIMIT),
        cost_estimate=cost(SMOOTH_COST),
        name="smooth_inner",
    )(own)


def smooth_outer(side, own, near, far, chunk):
    _, rates, width = own.shape
    wide = width // CHUNKS
    outs = [jax.ShapeDtypeStruct((n, 2 * EDGE, wide), F32) for n in (WIDE, rates - WIDE)]
    return pl.pallas_call(
        outer_kernel,
        grid=(1,),
        out_shape=outs,
        in_specs=[SMEM] + [block(a, wide, chunk) for a in (own, near, far)],
        out_specs=[block(o, wide, 0) for o in outs],
        compiler_params=pltpu.CompilerParams(vmem_limit_bytes=VMEM_LIMIT),
        cost_estimate=cost(SMOOTH_COST),
        name="smooth_outer",
    )(side, own, near, far)


def settle_kernel(plan, *refs):
    parts, vols, rates, first, last, low, high, k_low, k_high, whole, aliased, waits = plan
    refs = list(refs)
    side = refs.pop(0)
    sources = [refs.pop(0) for _ in range(parts)]
    left_node, left_hi, left_lo, right_hi, right_lo, growth, felicity = [refs.pop(0) for _ in range(7)]
    carried = None if first else (refs.pop(0), refs.pop(0))
    del refs[: aliased + waits]
    outs = [refs.pop(0) for _ in range(1 if whole else 2)]
    handed = None if last else (refs.pop(0), refs.pop(0))
    if whole:
        result = refs.pop(0)
        sem = refs.pop(0)
    windows, turned = refs
    tiles = high - low
    rows = rates * vols
    lane = lax.broadcasted_iota(jnp.int32, (rows, LANES), 1)
    base = 0 if first else 1

    def put(slot, value):
        hi = value.astype(BF16)
        lo = (value - hi.astype(F32)).astype(BF16)
        windows[0:rows, lanes_of(slot)] = hi
        windows[rows:, lanes_of(slot)] = lo

    vol_start, vol_end, at_start, at_end = [side[i] != 0 for i in range(1, 5)]
    if whole:
        edges = [at_start if e < REACH else at_end for e in range(rates + WIDE)]

        def beyond(i, e):
            return e < REACH or e >= rates + REACH

        def layers_of(at):
            return [ref[i, :, at] for ref in sources for i in range(ref.shape[0])]

    else:
        edges = [at_end] * (rates + WIDE)

        def beyond(i, e):
            return (e < rates) != (i < rates - REACH)

        def layers_of(at):
            inner = [ref[i, :, at] for ref in sources[: parts // 2] for i in range(ref.shape[0])]
            outer = [ref[i, :, at] for ref in sources[parts // 2 :] for i in range(ref.shape[0])]
            return [jnp.concatenate([o[:EDGE], n, o[EDGE:]], axis=0) for n, o in zip(inner, outer)]

    if first:
        turned[...] = jnp.zeros_like(turned)
    else:
        windows[:, 0:LANES] = carried[0][...]
        turned[...] = carried[1][...]

    def smooth(tile):
        layers = layers_of(lanes_of(tile))
        kept = [jnp.where(edge, 0.0, layer) for edge, layer in zip(edges, layers)]
        totals = []
        for i in range(rates):
            used = [kept[e] if beyond(i, e) else layers[e] for e in range(i, i + WIDE + 1)]
            total = (SCALE * GAUSS[REACH]) * used[REACH]
            for j in range(REACH):
                total = total + (SCALE * GAUSS[j]) * (used[j] + used[WIDE - j])
            totals.append(total)
        now = pltpu.roll(jnp.concatenate(totals, axis=0), LANES // 2, 1)
        put(tile + base, jnp.where(lane < LANES // 2, turned[...], now))
        turned[...] = now

    repeat(tiles, 4, smooth)
    if last:
        put(tiles + base, jnp.where(lane < LANES // 2, turned[...], 0.0))
    else:
        handed[0][...] = windows[:, lanes_of(tiles + base - 1)]
        handed[1][...] = turned[...]

    depth = lax.broadcasted_iota(jnp.int16, (2 * LANES, LANES), 0)
    nothing = jnp.zeros((2 * LANES, LANES), BF16)
    allocations = left_node.shape[0]

    def choose(tile):
        at = lanes_of(tile + k_low)
        here = lanes_of(tile)
        window = windows[:, lanes_of(tile, 2)]
        total = jnp.zeros((rates, vols, LANES), F32)
        for pair in range(0, allocations, 2):
            his, los = [], []
            for a in (pair, pair + 1):
                node = left_node[a : a + 1, at].astype(jnp.int16)
                is_left = depth == node
                is_right = depth == node + jnp.int16(1)
                his.append(jnp.where(is_left, left_hi[a : a + 1, at], jnp.where(is_right, right_hi[a : a + 1, at], nothing)))
                los.append(jnp.where(is_left, left_lo[a : a + 1, at], jnp.where(is_right, right_lo[a : a + 1, at], nothing)))
            both = jnp.dot(window, jnp.concatenate(his, axis=1), preferred_element_type=F32)
            rest = jnp.dot(window[:rows], jnp.concatenate(los, axis=1), preferred_element_type=F32)
            cont = both[:rows] + both[rows:] + rest
            for q in (0, 1):
                power = jnp.exp2(cont[:, q * LANES : (q + 1) * LANES].reshape(rates, vols, LANES))
                total = total + growth[pair + q] * power
        value = (SMOOTHING * LN2) * jnp.log2(total) + felicity[0:1, at]
        value = jnp.swapaxes(value, 0, 1)
        if whole:
            result[:, :, here] = value
        else:
            half = EDGE // 2
            rows_in = [value[i] for i in range(1, vols - 1)]
            rows_in = (
                [jnp.where(vol_start, 0.0, r) for r in rows_in[: half - 1]]
                + rows_in[half - 1 : 1 - half]
                + [jnp.where(vol_end, 0.0, r) for r in rows_in[1 - half :]]
            )
            onward = jnp.swapaxes(jnp.stack(smooth_rows(rows_in)), 0, 1)
            outs[0][:, :, here] = onward[: rates - WIDE]
            outs[1][:, :, here] = onward[rates - WIDE :]

    repeat(k_high - k_low, 4, choose)
    if whole:
        copy = pltpu.make_async_copy(result, outs[0].at[:, :, pl.ds(k_low * LANES, (k_high - k_low) * LANES)], sem)
        copy.start()
        copy.wait()


def cuts_of(section, index, tiles):
    step = tiles // CHUNKS
    low, high = index * step, (index + 1) * step
    first, last = index == 0, index == CHUNKS - 1
    low, high = (low if first else low - section), (high if last else high - section)
    return low, high, (0 if first else low - 1), (high if last else high - 1)


def settle(side, sources, specs, section, index, tables, growth, carried, out_so_far=None, after=()):
    whole = section == 1
    allocations, wealth = tables[0].shape
    low, high, k_low, k_high = cuts_of(section, index, wealth // LANES)
    first, last = index == 0, index == CHUNKS - 1
    vols = growth.shape[1]
    rates = out_so_far[0] if first and whole else None
    rates = 8 if rates is None else rates
    rows = vols * rates
    count = k_high - k_low
    full = lambda shape: pl.BlockSpec(shape, lambda i: (0,) * len(shape))
    operands = [side, *sources, *tables[:5], growth, tables[5]]
    specs = [SMEM, *specs] + [full(o.shape) for o in operands[1 + len(sources) :]]
    if not first:
        operands += list(carried)
        specs += [full(c.shape) for c in carried]
    aliases = {}
    aliased = whole and not first
    if aliased:
        aliases = {len(operands): 0}
        operands.append(out_so_far)
        specs.append(pl.BlockSpec(memory_space=pl.ANY))
    operands += list(after)
    specs += [pl.BlockSpec(memory_space=pl.ANY)] * len(after)
    scratch = []
    if whole:
        outs = [jax.ShapeDtypeStruct((vols, rates, wealth), F32)]
        out_specs = [pl.BlockSpec(memory_space=pl.ANY)]
        scratch += [pltpu.VMEM((vols, rates, count * LANES), F32), pltpu.SemaphoreType.DMA]
    else:
        outs = [jax.ShapeDtypeStruct((n, vols - EDGE, count * LANES), F32) for n in (rates - WIDE, WIDE)]
        out_specs = [full(o.shape) for o in outs]
    cut = len(outs)
    if not last:
        more = [jax.ShapeDtypeStruct((2 * rows, LANES), BF16), jax.ShapeDtypeStruct((rows, LANES), F32)]
        outs += more
        out_specs += [full(o.shape) for o in more]
    slots = (high - low) + (0 if first else 1) + (1 if last else 0)
    scratch += [pltpu.VMEM((2 * rows, slots * LANES), BF16), pltpu.VMEM((rows, LANES), F32)]
    plan = (len(sources), vols, rates, first, last, low, high, k_low, k_high, whole, aliased, len(after))
    got = pl.pallas_call(
        functools.partial(settle_kernel, plan),
        grid=(1,),
        out_shape=outs,
        in_specs=specs,
        out_specs=out_specs,
        scratch_shapes=scratch,
        input_output_aliases=aliases,
        compiler_params=pltpu.CompilerParams(vmem_limit_bytes=VMEM_LIMIT),
        cost_estimate=cost(SETTLE_COST),
        name="settle",
    )(*operands)
    return got[:cut], got[cut:]


def parts_of(x):
    hi = lax.reduce_precision(x, 8, 7)
    return hi.astype(BF16), (x - hi).astype(BF16)


def on_device(value_next, risk_cost, band_start, band_weight, felicity_array):
    vols, rates, wealth = value_next.shape
    vol_count, rate_count = lax.axis_size("vol"), lax.axis_size("rate")
    vol_at, rate_at = lax.axis_index("vol"), lax.axis_index("rate")
    paired = [(i, i ^ 1) for i in range(vol_count)]
    across = [(i, ((i + 1) ^ 1) - 1) for i in range(1, vol_count - 1)]
    rate_back = [(i, (i - 1) % rate_count) for i in range(rate_count)]
    rate_on = [(i, (i + 1) % rate_count) for i in range(rate_count)]

    core = vol_at % 2
    flags = [core == 0, vol_at == 0, vol_at == vol_count - 1, rate_at == 0, rate_at == rate_count - 1]
    side = jnp.stack(flags).astype(jnp.int32)

    risk_rows = jnp.pad(risk_cost.T[:, :, None], ((0, 0), (0, 0), (0, LANES - 1)))
    near_at = jnp.where(core == 0, vols - WIDE, 0)
    near, far = [
        jnp.concatenate([lax.dynamic_slice_in_dim(a, at, WIDE, axis=0) for a in (value_next, risk_rows)], axis=2)
        for at in (near_at, vols - WIDE - near_at)
    ]
    far = lax.ppermute(far, "vol", across)
    near = lax.ppermute(near, "vol", paired)

    inner = smooth_inner(value_next)
    inner = (*inner, lax.ppermute(inner[0], "rate", rate_back))
    outer = [smooth_outer(side, value_next, near, far, c) for c in range(CHUNKS)]
    outer = [(*o, lax.ppermute(o[0], "rate", rate_back)) for o in outer]

    window_start = (lax.broadcasted_iota(jnp.int32, band_start.shape, 1) // LANES) * LANES - LANES // 2
    tables = (band_start - window_start, *parts_of(1.0 - band_weight), *parts_of(band_weight), felicity_array[None, :])
    near_risk, far_risk = [a[:, :, wealth].T for a in (near, far)]
    low_risk = jnp.where(core == 0, far_risk, near_risk)[:, WIDE - EDGE // 2 :]
    high_risk = jnp.where(core == 0, near_risk, far_risk)[:, : EDGE // 2]
    growth_here, growth_wide = [
        jnp.broadcast_to(jnp.exp(r * (-1.0 / SMOOTHING))[:, :, None], (*r.shape, LANES))
        for r in (risk_cost, jnp.concatenate([low_risk, risk_cost, high_risk], axis=1))
    ]

    wide = wealth // CHUNKS
    onward, carried = [], None
    for c in range(CHUNKS):
        sources = (*inner, *outer[c])
        specs = [block(a, wide, c) for a in inner] + [block(a, wide, 0) for a in outer[c]]
        pieces, carried = settle(side, sources, specs, 0, c, tables, growth_wide, carried)
        onward.append((lax.ppermute(pieces[1], "rate", rate_on), *pieces))

    out, carried = (rates,), None
    for c in range(CHUNKS):
        specs = [block(a, a.shape[2], 0) for a in onward[c]]
        (out,), carried = settle(side, onward[c], specs, 1, c, tables, growth_here, carried, out)
    return out


def solution(mesh):
    return jax.shard_map(
        on_device,
        mesh=mesh,
        in_specs=(P("vol", "rate", None), P(None, "vol"), P(), P(), P()),
        out_specs=P("vol", "rate", None),
        check_vma=False,
    )
```

time: 913 us -> 59.8 us (0.07)
  local copies, waits for them, and re-layouts: 825 us -> 3.97 us
  Pallas kernels: 0 us -> 23 us
  waiting for transfers between devices: 38.7 us -> 18.3 us
  other arithmetic: 19.6 us -> 1.04 us
    gather x64 -> x0, local copies, waits for them, and re-layouts: 807 us -> none  [the longest x32 404 us: settle(): higher_node = jnp.take(expected, band_start[option] + 1, axis=2)]
    pallas_call x0 -> x13, Pallas kernels: none -> 23 us  [the longest x8 19.7 us: settle(): pl.pallas_call(functools.partial(settle_kernel, plan), grid=(1,), out_sha...]
    ppermute x8 -> x11, waiting for transfers between devices: 38.7 us -> 18.3 us  [the longest x1 8.22 us: on_device(): far = lax.ppermute(far, 'vol', across)]
    add x6 -> x0, other arithmetic: 19.4 us -> none  [the longest x2 14.4 us: settle(): smoothing_coefficient * jnp.log(normalizer_sum)]
    add x2 -> x0, local copies, waits for them, and re-layouts: 10.1 us -> none  [narrow(): result + hermite_weights[start_shift] * lax.slice_in_dim(padded, start_sh...]
    ppermute x8 -> x11, starting transfers between devices: 20.3 us -> 12.8 us  [the longest x1 4.75 us: on_device(): inner = (*inner, lax.ppermute(inner[0], 'rate', rate_back))]
  transfers between devices with their start and end apart: 8 -> 11, of which waited for: 7 -> 8; matrix products, arithmetic and copies ran while one was open for 1% -> 3% of each run, Pallas kernels for 0% -> 33%
where the time goes in v1:
time: 59.8 us; the launch traced here: 59.5 us
  Pallas kernels  23 us (38%)
  waiting for transfers between devices  18.3 us (31%)
  starting transfers between devices  12.8 us (21%)
  local copies, waits for them, and re-layouts  3.97 us (7%)
  other arithmetic  1.04 us (2%)
    pallas_call x8, Pallas kernels, settle(): pl.pallas_call(functools.partial(settle_kernel, plan), grid=(1,), out_sha...  19.7 us
    ppermute x1, waiting for transfers between devices, on_device(): far = lax.ppermute(far, 'vol', across)  8.22 us
    ppermute x4, waiting for transfers between devices, on_device(): outer = [(*o, lax.ppermute(o[0], 'rate', rate_back)) for o in outer]  7.03 us
    ppermute x1, starting transfers between devices, on_device(): inner = (*inner, lax.ppermute(inner[0], 'rate', rate_back))  4.75 us
    ppermute x1, starting transfers between devices, on_device(): far = lax.ppermute(far, 'vol', across)  3.91 us
    unnamed x12, local copies, waits for them, and re-layouts  3.34 us
    ppermute x4, waiting for transfers between devices, on_device(): onward.append((lax.ppermute(pieces[1], 'rate', rate_on), *pieces))  3.03 us
    pallas_call x4, Pallas kernels, smooth_outer(): pl.pallas_call(outer_kernel, grid=(1,), out_shape=outs, in_specs=[SMEM] +...  2.76 us
  transfers between devices with their start and end apart: 11, of which 8 were waited for; matrix products, arithmetic and copies ran while one was open for 3% of the time, Pallas kernels for 33%

profile of v1, /device:TPU:25, one launch (start us, length us, event | category | flops | bytes accessed | tf_op | source)
XLA Modules:
  0.0 59.5 jit_solution(16886802211232709430)
XLA Ops:
  0.0 1.2 %copy-done = f32[16,8,2048]{2,1,0:T(8,128)S(1)} copy-done((f32[16,8,2048]{2,1,0:T(8,128)S(1)}, f32[16,8,2048]{2,1,0:T(8,128)}, u32[]{:S(2)}) %copy-start) | copy-done | bytes 1048600
  1.2 0.5 smooth_inner.1
  1.8 4.8 %collective-permute-start = (f32[6,8,2048]{2,1,0:T(8,128)S(1)}, f32[6,8,2048]{2,1,0:T(8,128)S(1)}, u32[]{:S(2)}, u32[]{:S(2)}) collective-permute-start(f32[6,8,2048]{2,1,0:T(8,128)S(1)} %get-tuple-element.38.refs_1_), channel_id=1, source_target_pairs={{0,7},{1,0},{2,1},{3,2},{4,3},{5,4},{6,5},{7,6},{8,15},{9,8},{10,9... | collective-permute-start | bytes 1179656 | tf_op jit(solution)/shard_map/ppermute | solution.py:358
  6.5 0.7 %copy-done.5 = f32[8,16]{1,0:T(8,128)S(1)} copy-done((f32[8,16]{1,0:T(8,128)S(1)}, f32[8,16]{1,0:T(8,128)}, u32[]{:S(2)}) %copy-start.5) | copy-done | bytes 536
  7.2 0.1 copy.12
  7.3 0.1 constant_dynamic-slice_fusion
  7.5 1.0 %collective-permute-start.1 = (f32[6,8,2176]{2,1,0:T(8,128)S(1)}, f32[6,8,2176]{2,1,0:T(8,128)S(1)}, u32[]{:S(2)}, u32[]{:S(2)}) collective-permute-start(f32[6,8,2176]{2,1,0:T(8,128)S(1)} %pad_maximum_fusion), channel_id=1, source_target_pairs={{0,8},{8,0},{16,24},{24,16},{32,40},{40,32},{48,56},{56,48},{64,72... | collective-permute-start | bytes 1253384 | tf_op jit(solution)/shard_map/ppermute | solution.py:355
  8.5 0.8 %pad_maximum_fusion.1 = f32[6,8,2176]{2,1,0:T(8,128)} fusion(f32[6,8,128]{2,1,0:T(8,128)S(1)} %get-tuple-element.79, f32[6,8,2048]{2,1,0:T(8,128)S(1)} %get-tuple-element.73), kind=kLoop, calls=%fused_computation.1 | loop fusion | flops 104448 | bytes 835584 | tf_op jit(solution)/shard_map/concatenate | solution.py:351
  9.3 3.9 %collective-permute-start.2 = (f32[6,8,2176]{2,1,0:T(8,128)}, f32[6,8,2176]{2,1,0:T(8,128)S(1)}, u32[]{:S(2)}, u32[]{:S(2)}) collective-permute-start(f32[6,8,2176]{2,1,0:T(8,128)} %pad_maximum_fusion.1), channel_id=1, source_target_pairs={{8,16},{16,8},{24,32},{32,24},{40,48},{48,40},{56,64},{64,56},{72,... | collective-permute-start | bytes 1253384 | tf_op jit(solution)/shard_map/ppermute | solution.py:354
  13.3 0.1 stack.23
  13.4 0.8 %copy-done.4 = s32[8,2048]{1,0:T(8,128)S(1)} copy-done((s32[8,2048]{1,0:T(8,128)S(1)}, s32[8,2048]{1,0:T(8,128)}, u32[]{:S(2)}) %copy-start.4) | copy-done | bytes 65560
  14.3 0.0 collective-permute-done.1.near
  14.3 8.2 %collective-permute-done.2.far = f32[6,8,2176]{2,1,0:T(8,128)S(1)} collective-permute-done((f32[6,8,2176]{2,1,0:T(8,128)}, f32[6,8,2176]{2,1,0:T(8,128)S(1)}, u32[]{:S(2)}, u32[]{:S(2)}) %collective-permute-start.2) | collective-permute-done | bytes 417824 | tf_op jit(solution)/shard_map/ppermute | solution.py:354
  22.5 0.1 select_reduce_fusion.1
  22.6 0.1 copy.14
  22.7 0.1 copy.13
  22.8 0.7 %smooth_outer.7 = (f32[6,16,512]{2,1,0:T(8,128)S(1)}, f32[2,16,512]{2,1,0:T(8,128)S(1)}) custom-call(s32[5]{0:T(128)S(1)} %convert_element_type.17.side.refs_0_, f32[16,8,2048]{2,1,0:T(8,128)S(1)} %copy-done.1, f32[6,8,2176]{2,1,0:T(8,128)S(1)} %collective-permute-done.1.near, f32[6,8,2176]{2,1,0:T(8,128)S(1)} %collective-permute-done.2.far), custom_call_target="tpu_custom_call" | custom-call | flops 1000000000 | tf_op jit(solution)/shard_map/smooth_outer/pallas_call | solution.py:136
  23.5 0.3 collective-permute-start.6
  23.8 0.7 %smooth_outer.6 = (f32[6,16,512]{2,1,0:T(8,128)S(1)}, f32[2,16,512]{2,1,0:T(8,128)S(1)}) custom-call(s32[5]{0:T(128)S(1)} %convert_element_type.17.side.refs_0_, f32[16,8,2048]{2,1,0:T(8,128)S(1)} %copy-done.1, f32[6,8,2176]{2,1,0:T(8,128)S(1)} %collective-permute-done.1.near, f32[6,8,2176]{2,1,0:T(8,128)S(1)} %collective-permute-done.2.far), custom_call_target="tpu_custom_call" | custom-call | flops 1000000000 | tf_op jit(solution)/shard_map/smooth_outer/pallas_call | solution.py:136
  24.5 1.1 %collective-permute-start.5 = (f32[6,16,512]{2,1,0:T(8,128)S(1)}, f32[6,16,512]{2,1,0:T(8,128)S(1)}, u32[]{:S(2)}, u32[]{:S(2)}) collective-permute-start(f32[6,16,512]{2,1,0:T(8,128)S(1)} %get-tuple-element.44.refs_4_), channel_id=1, source_target_pairs={{0,7},{1,0},{2,1},{3,2},{4,3},{5,4},{6,5},{7,6},{8,15},{9,8},{10,9... | collective-permute-start | bytes 589832 | tf_op jit(solution)/shard_map/ppermute | solution.py:360
  25.6 0.7 %smooth_outer.5 = (f32[6,16,512]{2,1,0:T(8,128)S(1)}, f32[2,16,512]{2,1,0:T(8,128)S(1)}) custom-call(s32[5]{0:T(128)S(1)} %convert_element_type.17.side.refs_0_, f32[16,8,2048]{2,1,0:T(8,128)S(1)} %copy-done.1, f32[6,8,2176]{2,1,0:T(8,128)S(1)} %collective-permute-done.1.near, f32[6,8,2176]{2,1,0:T(8,128)S(1)} %collective-permute-done.2.far), custom_call_target="tpu_custom_call" | custom-call | flops 1000000000 | tf_op jit(solution)/shard_map/smooth_outer/pallas_call | solution.py:136
  26.3 0.3 collective-permute-start.4
  26.6 0.7 %smooth_outer.4 = (f32[6,16,512]{2,1,0:T(8,128)S(1)}, f32[2,16,512]{2,1,0:T(8,128)S(1)}) custom-call(s32[5]{0:T(128)S(1)} %convert_element_type.17.side.refs_0_, f32[16,8,2048]{2,1,0:T(8,128)S(1)} %copy-done.1, f32[6,8,2176]{2,1,0:T(8,128)S(1)} %collective-permute-done.1.near, f32[6,8,2176]{2,1,0:T(8,128)S(1)} %collective-permute-done.2.far), custom_call_target="tpu_custom_call" | custom-call | flops 1000000000 | tf_op jit(solution)/shard_map/smooth_outer/pallas_call | solution.py:136
  27.3 0.8 %collective-permute-start.3 = (f32[6,16,512]{2,1,0:T(8,128)S(1)}, f32[6,16,512]{2,1,0:T(8,128)S(1)}, u32[]{:S(2)}, u32[]{:S(2)}) collective-permute-start(f32[6,16,512]{2,1,0:T(8,128)S(1)} %get-tuple-element.40.refs_4_), channel_id=1, source_target_pairs={{0,7},{1,0},{2,1},{3,2},{4,3},{5,4},{6,5},{7,6},{8,15},{9,8},{10,9... | collective-permute-start | bytes 589832 | tf_op jit(solution)/shard_map/ppermute | solution.py:360
  28.1 0.1 fusion.5
  28.2 2.3 %collective-permute-done.6.refs_6_ = f32[6,16,512]{2,1,0:T(8,128)S(1)} collective-permute-done((f32[6,16,512]{2,1,0:T(8,128)S(1)}, f32[6,16,512]{2,1,0:T(8,128)S(1)}, u32[]{:S(2)}, u32[]{:S(2)}) %collective-permute-start.6) | collective-permute-done | bytes 196640 | tf_op jit(solution)/shard_map/ppermute | solution.py:360
  30.5 0.1 broadcast_in_dim.9.refs_12_
  30.6 0.6 %copy-done.2 = f32[2048]{0:T(1024)S(1)} copy-done((f32[2048]{0:T(1024)S(1)}, f32[2048]{0:T(1024)}, u32[]{:S(2)}) %copy-start.2) | copy-done | bytes 8216
  31.2 2.1 %settle.8 = (f32[2,16,384]{2,1,0:T(8,128)S(1)}, f32[6,16,384]{2,1,0:T(8,128)S(1)}, bf16[384,128]{1,0:T(8,128)(2,1)S(1)}, f32[192,128]{1,0:T(8,128)S(1)}) custom-call(s32[5]{0:T(128)S(1)} %convert_element_type.17.side.refs_0_, f32[6,8,2048]{2,1,0:T(8,128)S(1)} %get-tuple-element.38.refs_1_, f32[2,8,2048]{2,1,0:T(8,128)S(1)} %get-tuple-element.39.refs_2_, ...), custom_call_target="tpu_custom_call" | custom-call | flops 4000000000 | tf_op jit(solution)/shard_map/settle/pallas_call | solution.py:315
  33.3 0.1 collective-permute-start.10
  33.4 1.3 %collective-permute-done.5.refs_6_ = f32[6,16,512]{2,1,0:T(8,128)S(1)} collective-permute-done((f32[6,16,512]{2,1,0:T(8,128)S(1)}, f32[6,16,512]{2,1,0:T(8,128)S(1)}, u32[]{:S(2)}, u32[]{:S(2)}) %collective-permute-start.5) | collective-permute-done | bytes 196640 | tf_op jit(solution)/shard_map/ppermute | solution.py:360
  34.7 2.4 %settle.9 = (f32[2,16,512]{2,1,0:T(8,128)S(1)}, f32[6,16,512]{2,1,0:T(8,128)S(1)}, bf16[384,128]{1,0:T(8,128)(2,1)S(1)}, f32[192,128]{1,0:T(8,128)S(1)}) custom-call(s32[5]{0:T(128)S(1)} %convert_element_type.17.side.refs_0_, f32[6,8,2048]{2,1,0:T(8,128)S(1)} %get-tuple-element.38.refs_1_, f32[2,8,2048]{2,1,0:T(8,128)S(1)} %get-tuple-element.39.refs_2_, ...), custom_call_target="tpu_custom_call" | custom-call | flops 4000000000 | tf_op jit(solution)/shard_map/settle/pallas_call | solution.py:315
  37.2 0.1 collective-permute-start.9
  37.2 1.7 %collective-permute-done.4.refs_6_ = f32[6,16,512]{2,1,0:T(8,128)S(1)} collective-permute-done((f32[6,16,512]{2,1,0:T(8,128)S(1)}, f32[6,16,512]{2,1,0:T(8,128)S(1)}, u32[]{:S(2)}, u32[]{:S(2)}) %collective-permute-start.4) | collective-permute-done | bytes 196640 | tf_op jit(solution)/shard_map/ppermute | solution.py:360
  38.9 2.4 %settle.10 = (f32[2,16,512]{2,1,0:T(8,128)S(1)}, f32[6,16,512]{2,1,0:T(8,128)S(1)}, bf16[384,128]{1,0:T(8,128)(2,1)S(1)}, f32[192,128]{1,0:T(8,128)S(1)}) custom-call(s32[5]{0:T(128)S(1)} %convert_element_type.17.side.refs_0_, f32[6,8,2048]{2,1,0:T(8,128)S(1)} %get-tuple-element.38.refs_1_, f32[2,8,2048]{2,1,0:T(8,128)S(1)} %get-tuple-element.39.refs_2_, ...), custom_call_target="tpu_custom_call" | custom-call | flops 4000000000 | tf_op jit(solution)/shard_map/settle/pallas_call | solution.py:315
  41.4 0.1 collective-permute-start.8
  41.4 1.7 %collective-permute-done.3.refs_6_ = f32[6,16,512]{2,1,0:T(8,128)S(1)} collective-permute-done((f32[6,16,512]{2,1,0:T(8,128)S(1)}, f32[6,16,512]{2,1,0:T(8,128)S(1)}, u32[]{:S(2)}, u32[]{:S(2)}) %collective-permute-start.3) | collective-permute-done | bytes 196640 | tf_op jit(solution)/shard_map/ppermute | solution.py:360
  43.1 2.8 %settle.11 = (f32[2,16,640]{2,1,0:T(8,128)S(1)}, f32[6,16,640]{2,1,0:T(8,128)S(1)}) custom-call(s32[5]{0:T(128)S(1)} %convert_element_type.17.side.refs_0_, f32[6,8,2048]{2,1,0:T(8,128)S(1)} %get-tuple-element.38.refs_1_, f32[2,8,2048]{2,1,0:T(8,128)S(1)} %get-tuple-element.39.refs_2_, f32[6,8,2048]{2,1,0:T(8,128)S(1)} %collective-permute-done.refs_3_, ...), custom_call_target="tpu_custom_call" | custom-call | flops 4000000000 | tf_op jit(solution)/shard_map/settle/pallas_call | solution.py:315
  45.9 0.3 collective-permute-start.7
  46.2 0.0 collective-permute-done.10.refs_1_
  46.2 0.1 broadcast_in_dim.21.refs_9_
  46.3 2.0 %settle.12 = (f32[16,8,2048]{2,1,0:T(8,128)}, bf16[256,128]{1,0:T(8,128)(2,1)S(1)}, f32[128,128]{1,0:T(8,128)S(1)}) custom-call(s32[5]{0:T(128)S(1)} %convert_element_type.17.side.refs_0_, f32[6,16,384]{2,1,0:T(8,128)S(1)} %collective-permute-done.10.refs_1_, f32[2,16,384]{2,1,0:T(8,128)S(1)} %get-tuple-element.61.refs_2_, ...), custom_call_target="tpu_custom_call" | custom-call | flops 4000000000 | tf_op jit(solution)/shard_map/settle/pallas_call | solution.py:315
  48.3 2.1 %collective-permute-done.9.refs_1_ = f32[6,16,512]{2,1,0:T(8,128)S(1)} collective-permute-done((f32[6,16,512]{2,1,0:T(8,128)S(1)}, f32[6,16,512]{2,1,0:T(8,128)S(1)}, u32[]{:S(2)}, u32[]{:S(2)}) %collective-permute-start.9) | collective-permute-done | bytes 196640 | tf_op jit(solution)/shard_map/ppermute | solution.py:378
  50.4 2.5 %settle.13 = (f32[16,8,2048]{2,1,0:T(8,128)}, bf16[256,128]{1,0:T(8,128)(2,1)S(1)}, f32[128,128]{1,0:T(8,128)S(1)}) custom-call(s32[5]{0:T(128)S(1)} %convert_element_type.17.side.refs_0_, f32[6,16,512]{2,1,0:T(8,128)S(1)} %collective-permute-done.9.refs_1_, f32[2,16,512]{2,1,0:T(8,128)S(1)} %get-tuple-element.59.refs_2_, ...), custom_call_target="tpu_custom_call", output_to_operand_aliasing={{0}: (13, {})} | custom-call | flops 4000000000 | tf_op jit(solution)/shard_map/settle/pallas_call | solution.py:315
  52.9 0.8 %collective-permute-done.8.refs_1_ = f32[6,16,512]{2,1,0:T(8,128)S(1)} collective-permute-done((f32[6,16,512]{2,1,0:T(8,128)S(1)}, f32[6,16,512]{2,1,0:T(8,128)S(1)}, u32[]{:S(2)}, u32[]{:S(2)}) %collective-permute-start.8) | collective-permute-done | bytes 196640 | tf_op jit(solution)/shard_map/ppermute | solution.py:378
  53.7 2.5 %settle.14 = (f32[16,8,2048]{2,1,0:T(8,128)}, bf16[256,128]{1,0:T(8,128)(2,1)S(1)}, f32[128,128]{1,0:T(8,128)S(1)}) custom-call(s32[5]{0:T(128)S(1)} %convert_element_type.17.side.refs_0_, f32[6,16,512]{2,1,0:T(8,128)S(1)} %collective-permute-done.8.refs_1_, f32[2,16,512]{2,1,0:T(8,128)S(1)} %get-tuple-element.57.refs_2_, ...), custom_call_target="tpu_custom_call", output_to_operand_aliasing={{0}: (13, {})} | custom-call | flops 4000000000 | tf_op jit(solution)/shard_map/settle/pallas_call | solution.py:315
  56.2 0.1 collective-permute-done.7.refs_1_
  56.3 3.0 %settle.15 = f32[16,8,2048]{2,1,0:T(8,128)} custom-call(s32[5]{0:T(128)S(1)} %convert_element_type.17.side.refs_0_, f32[6,16,640]{2,1,0:T(8,128)S(1)} %collective-permute-done.7.refs_1_, f32[2,16,640]{2,1,0:T(8,128)S(1)} %get-tuple-element.55.refs_2_, f32[6,16,640]{2,1,0:T(8,128)S(1)} %get-tuple-element.54.refs_3_, ...), custom_call_target="tpu_custom_call", output_to_operand_aliasing={{}: (13, {})} | custom-call | flops 4000000000 | tf_op jit(solution)/shard_map/settle/pallas_call | solution.py:315
  (19 shorter events, 0.1 us)
Async XLA Ops:
  0.0 1.2 %copy-start = (f32[16,8,2048]{2,1,0:T(8,128)S(1)}, f32[16,8,2048]{2,1,0:T(8,128)}, u32[]{:S(2)}) copy-start(f32[16,8,2048]{2,1,0:T(8,128)} %own.9) | copy-start | bytes 3145732
  1.2 6.1 %copy-start.1 = (f32[16,8,2048]{2,1,0:T(8,128)S(1)}, f32[16,8,2048]{2,1,0:T(8,128)}, u32[]{:S(2)}) copy-start(f32[16,8,2048]{2,1,0:T(8,128)} %own.9) | copy-start | bytes 3145732
  1.8 26.4 %collective-permute-start = (f32[6,8,2048]{2,1,0:T(8,128)S(1)}, f32[6,8,2048]{2,1,0:T(8,128)S(1)}, u32[]{:S(2)}, u32[]{:S(2)}) collective-permute-start(f32[6,8,2048]{2,1,0:T(8,128)S(1)} %get-tuple-element.38.refs_1_), channel_id=1, source_target_pairs={{0,7},{1,0},{2,1},{3,2},{4,3},{5,4},{6,5},{7,6},{8,15},{9,8},{10,9... | collective-permute-start | bytes 1179656 | tf_op jit(solution)/shard_map/ppermute | solution.py:358
  6.5 0.7 %copy-start.5 = (f32[8,16]{1,0:T(8,128)S(1)}, f32[8,16]{1,0:T(8,128)}, u32[]{:S(2)}) copy-start(f32[8,16]{1,0:T(8,128)} %param.6) | copy-start | bytes 1540
  7.5 6.8 %collective-permute-start.1 = (f32[6,8,2176]{2,1,0:T(8,128)S(1)}, f32[6,8,2176]{2,1,0:T(8,128)S(1)}, u32[]{:S(2)}, u32[]{:S(2)}) collective-permute-start(f32[6,8,2176]{2,1,0:T(8,128)S(1)} %pad_maximum_fusion), channel_id=1, source_target_pairs={{0,8},{8,0},{16,24},{24,16},{32,40},{40,32},{48,56},{56,48},{64,72... | collective-permute-start | bytes 1253384 | tf_op jit(solution)/shard_map/ppermute | solution.py:355
  8.5 4.9 %copy-start.3 = (f32[8,2048]{1,0:T(8,128)S(1)}, f32[8,2048]{1,0:T(8,128)}, u32[]{:S(2)}) copy-start(f32[8,2048]{1,0:T(8,128)} %param.8) | copy-start | bytes 196612
  9.3 13.2 %collective-permute-start.2 = (f32[6,8,2176]{2,1,0:T(8,128)}, f32[6,8,2176]{2,1,0:T(8,128)S(1)}, u32[]{:S(2)}, u32[]{:S(2)}) collective-permute-start(f32[6,8,2176]{2,1,0:T(8,128)} %pad_maximum_fusion.1), channel_id=1, source_target_pairs={{8,16},{16,8},{24,32},{32,24},{40,48},{48,40},{56,64},{64,56},{72,... | collective-permute-start | bytes 1253384 | tf_op jit(solution)/shard_map/ppermute | solution.py:354
  13.4 0.8 %copy-start.4 = (s32[8,2048]{1,0:T(8,128)S(1)}, s32[8,2048]{1,0:T(8,128)}, u32[]{:S(2)}) copy-start(s32[8,2048]{1,0:T(8,128)} %param.7) | copy-start | bytes 196612
  23.5 7.1 %collective-permute-start.6 = (f32[6,16,512]{2,1,0:T(8,128)S(1)}, f32[6,16,512]{2,1,0:T(8,128)S(1)}, u32[]{:S(2)}, u32[]{:S(2)}) collective-permute-start(f32[6,16,512]{2,1,0:T(8,128)S(1)} %get-tuple-element.46.refs_4_), channel_id=1, source_target_pairs={{0,7},{1,0},{2,1},{3,2},{4,3},{5,4},{6,5},{7,6},{8,15},{9,8},{10,9... | collective-permute-start | bytes 589832 | tf_op jit(solution)/shard_map/ppermute | solution.py:360
  24.5 10.3 %collective-permute-start.5 = (f32[6,16,512]{2,1,0:T(8,128)S(1)}, f32[6,16,512]{2,1,0:T(8,128)S(1)}, u32[]{:S(2)}, u32[]{:S(2)}) collective-permute-start(f32[6,16,512]{2,1,0:T(8,128)S(1)} %get-tuple-element.44.refs_4_), channel_id=1, source_target_pairs={{0,7},{1,0},{2,1},{3,2},{4,3},{5,4},{6,5},{7,6},{8,15},{9,8},{10,9... | collective-permute-start | bytes 589832 | tf_op jit(solution)/shard_map/ppermute | solution.py:360
  26.3 12.6 %collective-permute-start.4 = (f32[6,16,512]{2,1,0:T(8,128)S(1)}, f32[6,16,512]{2,1,0:T(8,128)S(1)}, u32[]{:S(2)}, u32[]{:S(2)}) collective-permute-start(f32[6,16,512]{2,1,0:T(8,128)S(1)} %get-tuple-element.42.refs_4_), channel_id=1, source_target_pairs={{0,7},{1,0},{2,1},{3,2},{4,3},{5,4},{6,5},{7,6},{8,15},{9,8},{10,9... | collective-permute-start | bytes 589832 | tf_op jit(solution)/shard_map/ppermute | solution.py:360
  27.3 15.8 %collective-permute-start.3 = (f32[6,16,512]{2,1,0:T(8,128)S(1)}, f32[6,16,512]{2,1,0:T(8,128)S(1)}, u32[]{:S(2)}, u32[]{:S(2)}) collective-permute-start(f32[6,16,512]{2,1,0:T(8,128)S(1)} %get-tuple-element.40.refs_4_), channel_id=1, source_target_pairs={{0,7},{1,0},{2,1},{3,2},{4,3},{5,4},{6,5},{7,6},{8,15},{9,8},{10,9... | collective-permute-start | bytes 589832 | tf_op jit(solution)/shard_map/ppermute | solution.py:360
  30.5 0.7 %copy-start.2 = (f32[2048]{0:T(1024)S(1)}, f32[2048]{0:T(1024)}, u32[]{:S(2)}) copy-start(f32[2048]{0:T(1024)} %param.9) | copy-start | bytes 24580
  33.3 12.9 %collective-permute-start.10 = (f32[6,16,384]{2,1,0:T(8,128)S(1)}, f32[6,16,384]{2,1,0:T(8,128)S(1)}, u32[]{:S(2)}, u32[]{:S(2)}) collective-permute-start(f32[6,16,384]{2,1,0:T(8,128)S(1)} %get-tuple-element.60.refs_3_), channel_id=1, source_target_pairs={{0,1},{1,2},{2,3},{3,4},{4,5},{5,6},{6,7},{7,0},{8,9},{9,10},{10,1... | collective-permute-start | bytes 442376 | tf_op jit(solution)/shard_map/ppermute | solution.py:378
  37.2 13.2 %collective-permute-start.9 = (f32[6,16,512]{2,1,0:T(8,128)S(1)}, f32[6,16,512]{2,1,0:T(8,128)S(1)}, u32[]{:S(2)}, u32[]{:S(2)}) collective-permute-start(f32[6,16,512]{2,1,0:T(8,128)S(1)} %get-tuple-element.58.refs_3_), channel_id=1, source_target_pairs={{0,1},{1,2},{2,3},{3,4},{4,5},{5,6},{6,7},{7,0},{8,9},{9,10},{10,1... | collective-permute-start | bytes 589832 | tf_op jit(solution)/shard_map/ppermute | solution.py:378
  41.4 12.3 %collective-permute-start.8 = (f32[6,16,512]{2,1,0:T(8,128)S(1)}, f32[6,16,512]{2,1,0:T(8,128)S(1)}, u32[]{:S(2)}, u32[]{:S(2)}) collective-permute-start(f32[6,16,512]{2,1,0:T(8,128)S(1)} %get-tuple-element.56.refs_3_), channel_id=1, source_target_pairs={{0,1},{1,2},{2,3},{3,4},{4,5},{5,6},{6,7},{7,0},{8,9},{9,10},{10,1... | collective-permute-start | bytes 589832 | tf_op jit(solution)/shard_map/ppermute | solution.py:378
  45.9 10.4 %collective-permute-start.7 = (f32[6,16,640]{2,1,0:T(8,128)S(1)}, f32[6,16,640]{2,1,0:T(8,128)S(1)}, u32[]{:S(2)}, u32[]{:S(2)}) collective-permute-start(f32[6,16,640]{2,1,0:T(8,128)S(1)} %get-tuple-element.54.refs_3_), channel_id=1, source_target_pairs={{0,1},{1,2},{2,3},{3,4},{4,5},{5,6},{6,7},{7,0},{8,9},{9,10},{10,1... | collective-permute-start | bytes 737288 | tf_op jit(solution)/shard_map/ppermute | solution.py:378

commit v2 on v1

--- a/solution.py
+++ b/solution.py
@@ -35,7 +35,7 @@
 
 SMEM = pl.BlockSpec(memory_space=pltpu.SMEM)
 VMEM = pl.BlockSpec(memory_space=pltpu.VMEM)
-VMEM_LIMIT = 24 * 2**20
+VMEM_LIMIT = 10 * 2**20
 
 
 def repeat(count, step, body):

time: 59.8 us -> 59.8 us (level)
  no operation moved by 1% of the time
where the time goes in v2:
time: 59.8 us; the launch traced here: 59.5 us
  Pallas kernels  23.1 us (39%)
  waiting for transfers between devices  18.3 us (31%)
  starting transfers between devices  12.8 us (21%)
  local copies, waits for them, and re-layouts  3.97 us (7%)
  other arithmetic  1.04 us (2%)
    pallas_call x8, Pallas kernels, settle(): pl.pallas_call(functools.partial(settle_kernel, plan), grid=(1,), out_sha...  19.8 us
    ppermute x1, waiting for transfers between devices, on_device(): far = lax.ppermute(far, 'vol', across)  8.22 us
    ppermute x4, waiting for transfers between devices, on_device(): outer = [(*o, lax.ppermute(o[0], 'rate', rate_back)) for o in outer]  7.02 us
    ppermute x1, starting transfers between devices, on_device(): inner = (*inner, lax.ppermute(inner[0], 'rate', rate_back))  4.75 us
    ppermute x1, starting transfers between devices, on_device(): far = lax.ppermute(far, 'vol', across)  3.91 us
    unnamed x12, local copies, waits for them, and re-layouts  3.34 us
    ppermute x4, waiting for transfers between devices, on_device(): onward.append((lax.ppermute(pieces[1], 'rate', rate_on), *pieces))  3.02 us
    pallas_call x4, Pallas kernels, smooth_outer(): pl.pallas_call(outer_kernel, grid=(1,), out_shape=outs, in_specs=[SMEM] +...  2.76 us
  transfers between devices with their start and end apart: 11, of which 8 were waited for; matrix products, arithmetic and copies ran while one was open for 3% of the time, Pallas kernels for 33%

profile of v2, /device:TPU:25, one launch (start us, length us, event | category | flops | bytes accessed | tf_op | source)
XLA Modules:
  0.0 59.5 jit_solution(7233597192844858437)
XLA Ops:
  0.0 1.2 %copy-done = f32[16,8,2048]{2,1,0:T(8,128)S(1)} copy-done((f32[16,8,2048]{2,1,0:T(8,128)S(1)}, f32[16,8,2048]{2,1,0:T(8,128)}, u32[]{:S(2)}) %copy-start) | copy-done | bytes 1048600
  1.2 0.5 smooth_inner.1
  1.8 4.8 %collective-permute-start = (f32[6,8,2048]{2,1,0:T(8,128)S(1)}, f32[6,8,2048]{2,1,0:T(8,128)S(1)}, u32[]{:S(2)}, u32[]{:S(2)}) collective-permute-start(f32[6,8,2048]{2,1,0:T(8,128)S(1)} %get-tuple-element.38.refs_1_), channel_id=1, source_target_pairs={{0,7},{1,0},{2,1},{3,2},{4,3},{5,4},{6,5},{7,6},{8,15},{9,8},{10,9... | collective-permute-start | bytes 1179656 | tf_op jit(solution)/shard_map/ppermute | solution.py:358
  6.5 0.7 %copy-done.5 = f32[8,16]{1,0:T(8,128)S(1)} copy-done((f32[8,16]{1,0:T(8,128)S(1)}, f32[8,16]{1,0:T(8,128)}, u32[]{:S(2)}) %copy-start.5) | copy-done | bytes 536
  7.2 0.1 copy.12
  7.3 0.1 constant_dynamic-slice_fusion
  7.5 1.0 %collective-permute-start.1 = (f32[6,8,2176]{2,1,0:T(8,128)S(1)}, f32[6,8,2176]{2,1,0:T(8,128)S(1)}, u32[]{:S(2)}, u32[]{:S(2)}) collective-permute-start(f32[6,8,2176]{2,1,0:T(8,128)S(1)} %pad_maximum_fusion), channel_id=1, source_target_pairs={{0,8},{8,0},{16,24},{24,16},{32,40},{40,32},{48,56},{56,48},{64,72... | collective-permute-start | bytes 1253384 | tf_op jit(solution)/shard_map/ppermute | solution.py:355
  8.5 0.8 %pad_maximum_fusion.1 = f32[6,8,2176]{2,1,0:T(8,128)} fusion(f32[6,8,128]{2,1,0:T(8,128)S(1)} %get-tuple-element.79, f32[6,8,2048]{2,1,0:T(8,128)S(1)} %get-tuple-element.73), kind=kLoop, calls=%fused_computation.1 | loop fusion | flops 104448 | bytes 835584 | tf_op jit(solution)/shard_map/concatenate | solution.py:351
  9.3 3.9 %collective-permute-start.2 = (f32[6,8,2176]{2,1,0:T(8,128)}, f32[6,8,2176]{2,1,0:T(8,128)S(1)}, u32[]{:S(2)}, u32[]{:S(2)}) collective-permute-start(f32[6,8,2176]{2,1,0:T(8,128)} %pad_maximum_fusion.1), channel_id=1, source_target_pairs={{8,16},{16,8},{24,32},{32,24},{40,48},{48,40},{56,64},{64,56},{72,... | collective-permute-start | bytes 1253384 | tf_op jit(solution)/shard_map/ppermute | solution.py:354
  13.3 0.1 stack.23
  13.4 0.8 %copy-done.4 = s32[8,2048]{1,0:T(8,128)S(1)} copy-done((s32[8,2048]{1,0:T(8,128)S(1)}, s32[8,2048]{1,0:T(8,128)}, u32[]{:S(2)}) %copy-start.4) | copy-done | bytes 65560
  14.3 0.0 collective-permute-done.1.near
  14.3 8.2 %collective-permute-done.2.far = f32[6,8,2176]{2,1,0:T(8,128)S(1)} collective-permute-done((f32[6,8,2176]{2,1,0:T(8,128)}, f32[6,8,2176]{2,1,0:T(8,128)S(1)}, u32[]{:S(2)}, u32[]{:S(2)}) %collective-permute-start.2) | collective-permute-done | bytes 417824 | tf_op jit(solution)/shard_map/ppermute | solution.py:354
  22.5 0.1 select_reduce_fusion.1
  22.6 0.1 copy.14
  22.7 0.1 copy.13
  22.8 0.7 %smooth_outer.7 = (f32[6,16,512]{2,1,0:T(8,128)S(1)}, f32[2,16,512]{2,1,0:T(8,128)S(1)}) custom-call(s32[5]{0:T(128)S(1)} %convert_element_type.17.side.refs_0_, f32[16,8,2048]{2,1,0:T(8,128)S(1)} %copy-done.1, f32[6,8,2176]{2,1,0:T(8,128)S(1)} %collective-permute-done.1.near, f32[6,8,2176]{2,1,0:T(8,128)S(1)} %collective-permute-done.2.far), custom_call_target="tpu_custom_call" | custom-call | flops 1000000000 | tf_op jit(solution)/shard_map/smooth_outer/pallas_call | solution.py:136
  23.5 0.3 collective-permute-start.6
  23.8 0.7 %smooth_outer.6 = (f32[6,16,512]{2,1,0:T(8,128)S(1)}, f32[2,16,512]{2,1,0:T(8,128)S(1)}) custom-call(s32[5]{0:T(128)S(1)} %convert_element_type.17.side.refs_0_, f32[16,8,2048]{2,1,0:T(8,128)S(1)} %copy-done.1, f32[6,8,2176]{2,1,0:T(8,128)S(1)} %collective-permute-done.1.near, f32[6,8,2176]{2,1,0:T(8,128)S(1)} %collective-permute-done.2.far), custom_call_target="tpu_custom_call" | custom-call | flops 1000000000 | tf_op jit(solution)/shard_map/smooth_outer/pallas_call | solution.py:136
  24.5 1.1 %collective-permute-start.5 = (f32[6,16,512]{2,1,0:T(8,128)S(1)}, f32[6,16,512]{2,1,0:T(8,128)S(1)}, u32[]{:S(2)}, u32[]{:S(2)}) collective-permute-start(f32[6,16,512]{2,1,0:T(8,128)S(1)} %get-tuple-element.44.refs_4_), channel_id=1, source_target_pairs={{0,7},{1,0},{2,1},{3,2},{4,3},{5,4},{6,5},{7,6},{8,15},{9,8},{10,9... | collective-permute-start | bytes 589832 | tf_op jit(solution)/shard_map/ppermute | solution.py:360
  25.6 0.7 %smooth_outer.5 = (f32[6,16,512]{2,1,0:T(8,128)S(1)}, f32[2,16,512]{2,1,0:T(8,128)S(1)}) custom-call(s32[5]{0:T(128)S(1)} %convert_element_type.17.side.refs_0_, f32[16,8,2048]{2,1,0:T(8,128)S(1)} %copy-done.1, f32[6,8,2176]{2,1,0:T(8,128)S(1)} %collective-permute-done.1.near, f32[6,8,2176]{2,1,0:T(8,128)S(1)} %collective-permute-done.2.far), custom_call_target="tpu_custom_call" | custom-call | flops 1000000000 | tf_op jit(solution)/shard_map/smooth_outer/pallas_call | solution.py:136
  26.3 0.3 collective-permute-start.4
  26.6 0.7 %smooth_outer.4 = (f32[6,16,512]{2,1,0:T(8,128)S(1)}, f32[2,16,512]{2,1,0:T(8,128)S(1)}) custom-call(s32[5]{0:T(128)S(1)} %convert_element_type.17.side.refs_0_, f32[16,8,2048]{2,1,0:T(8,128)S(1)} %copy-done.1, f32[6,8,2176]{2,1,0:T(8,128)S(1)} %collective-permute-done.1.near, f32[6,8,2176]{2,1,0:T(8,128)S(1)} %collective-permute-done.2.far), custom_call_target="tpu_custom_call" | custom-call | flops 1000000000 | tf_op jit(solution)/shard_map/smooth_outer/pallas_call | solution.py:136
  27.3 0.8 %collective-permute-start.3 = (f32[6,16,512]{2,1,0:T(8,128)S(1)}, f32[6,16,512]{2,1,0:T(8,128)S(1)}, u32[]{:S(2)}, u32[]{:S(2)}) collective-permute-start(f32[6,16,512]{2,1,0:T(8,128)S(1)} %get-tuple-element.40.refs_4_), channel_id=1, source_target_pairs={{0,7},{1,0},{2,1},{3,2},{4,3},{5,4},{6,5},{7,6},{8,15},{9,8},{10,9... | collective-permute-start | bytes 589832 | tf_op jit(solution)/shard_map/ppermute | solution.py:360
  28.1 0.1 fusion.5
  28.2 0.0 collective-permute-done.refs_3_
  28.2 2.3 %collective-permute-done.6.refs_6_ = f32[6,16,512]{2,1,0:T(8,128)S(1)} collective-permute-done((f32[6,16,512]{2,1,0:T(8,128)S(1)}, f32[6,16,512]{2,1,0:T(8,128)S(1)}, u32[]{:S(2)}, u32[]{:S(2)}) %collective-permute-start.6) | collective-permute-done | bytes 196640 | tf_op jit(solution)/shard_map/ppermute | solution.py:360
  30.5 0.1 broadcast_in_dim.9.refs_12_
  30.6 0.6 %copy-done.2 = f32[2048]{0:T(1024)S(1)} copy-done((f32[2048]{0:T(1024)S(1)}, f32[2048]{0:T(1024)}, u32[]{:S(2)}) %copy-start.2) | copy-done | bytes 8216
  31.2 2.1 %settle.8 = (f32[2,16,384]{2,1,0:T(8,128)S(1)}, f32[6,16,384]{2,1,0:T(8,128)S(1)}, bf16[384,128]{1,0:T(8,128)(2,1)S(1)}, f32[192,128]{1,0:T(8,128)S(1)}) custom-call(s32[5]{0:T(128)S(1)} %convert_element_type.17.side.refs_0_, f32[6,8,2048]{2,1,0:T(8,128)S(1)} %get-tuple-element.38.refs_1_, f32[2,8,2048]{2,1,0:T(8,128)S(1)} %get-tuple-element.39.refs_2_, ...), custom_call_target="tpu_custom_call" | custom-call | flops 4000000000 | tf_op jit(solution)/shard_map/settle/pallas_call | solution.py:315
  33.3 0.1 collective-permute-start.10
  33.4 1.3 %collective-permute-done.5.refs_6_ = f32[6,16,512]{2,1,0:T(8,128)S(1)} collective-permute-done((f32[6,16,512]{2,1,0:T(8,128)S(1)}, f32[6,16,512]{2,1,0:T(8,128)S(1)}, u32[]{:S(2)}, u32[]{:S(2)}) %collective-permute-start.5) | collective-permute-done | bytes 196640 | tf_op jit(solution)/shard_map/ppermute | solution.py:360
  34.7 2.4 %settle.9 = (f32[2,16,512]{2,1,0:T(8,128)S(1)}, f32[6,16,512]{2,1,0:T(8,128)S(1)}, bf16[384,128]{1,0:T(8,128)(2,1)S(1)}, f32[192,128]{1,0:T(8,128)S(1)}) custom-call(s32[5]{0:T(128)S(1)} %convert_element_type.17.side.refs_0_, f32[6,8,2048]{2,1,0:T(8,128)S(1)} %get-tuple-element.38.refs_1_, f32[2,8,2048]{2,1,0:T(8,128)S(1)} %get-tuple-element.39.refs_2_, ...), custom_call_target="tpu_custom_call" | custom-call | flops 4000000000 | tf_op jit(solution)/shard_map/settle/pallas_call | solution.py:315
  37.2 0.1 collective-permute-start.9
  37.2 1.7 %collective-permute-done.4.refs_6_ = f32[6,16,512]{2,1,0:T(8,128)S(1)} collective-permute-done((f32[6,16,512]{2,1,0:T(8,128)S(1)}, f32[6,16,512]{2,1,0:T(8,128)S(1)}, u32[]{:S(2)}, u32[]{:S(2)}) %collective-permute-start.4) | collective-permute-done | bytes 196640 | tf_op jit(solution)/shard_map/ppermute | solution.py:360
  38.9 2.4 %settle.10 = (f32[2,16,512]{2,1,0:T(8,128)S(1)}, f32[6,16,512]{2,1,0:T(8,128)S(1)}, bf16[384,128]{1,0:T(8,128)(2,1)S(1)}, f32[192,128]{1,0:T(8,128)S(1)}) custom-call(s32[5]{0:T(128)S(1)} %convert_element_type.17.side.refs_0_, f32[6,8,2048]{2,1,0:T(8,128)S(1)} %get-tuple-element.38.refs_1_, f32[2,8,2048]{2,1,0:T(8,128)S(1)} %get-tuple-element.39.refs_2_, ...), custom_call_target="tpu_custom_call" | custom-call | flops 4000000000 | tf_op jit(solution)/shard_map/settle/pallas_call | solution.py:315
  41.4 0.1 collective-permute-start.8
  41.5 1.7 %collective-permute-done.3.refs_6_ = f32[6,16,512]{2,1,0:T(8,128)S(1)} collective-permute-done((f32[6,16,512]{2,1,0:T(8,128)S(1)}, f32[6,16,512]{2,1,0:T(8,128)S(1)}, u32[]{:S(2)}, u32[]{:S(2)}) %collective-permute-start.3) | collective-permute-done | bytes 196640 | tf_op jit(solution)/shard_map/ppermute | solution.py:360
  43.1 2.8 %settle.11 = (f32[2,16,640]{2,1,0:T(8,128)S(1)}, f32[6,16,640]{2,1,0:T(8,128)S(1)}) custom-call(s32[5]{0:T(128)S(1)} %convert_element_type.17.side.refs_0_, f32[6,8,2048]{2,1,0:T(8,128)S(1)} %get-tuple-element.38.refs_1_, f32[2,8,2048]{2,1,0:T(8,128)S(1)} %get-tuple-element.39.refs_2_, f32[6,8,2048]{2,1,0:T(8,128)S(1)} %collective-permute-done.refs_3_, ...), custom_call_target="tpu_custom_call" | custom-call | flops 4000000000 | tf_op jit(solution)/shard_map/settle/pallas_call | solution.py:315
  45.9 0.3 collective-permute-start.7
  46.2 0.1 broadcast_in_dim.21.refs_9_
  46.3 2.0 %settle.12 = (f32[16,8,2048]{2,1,0:T(8,128)}, bf16[256,128]{1,0:T(8,128)(2,1)S(1)}, f32[128,128]{1,0:T(8,128)S(1)}) custom-call(s32[5]{0:T(128)S(1)} %convert_element_type.17.side.refs_0_, f32[6,16,384]{2,1,0:T(8,128)S(1)} %collective-permute-done.10.refs_1_, f32[2,16,384]{2,1,0:T(8,128)S(1)} %get-tuple-element.61.refs_2_, ...), custom_call_target="tpu_custom_call" | custom-call | flops 4000000000 | tf_op jit(solution)/shard_map/settle/pallas_call | solution.py:315
  48.3 2.1 %collective-permute-done.9.refs_1_ = f32[6,16,512]{2,1,0:T(8,128)S(1)} collective-permute-done((f32[6,16,512]{2,1,0:T(8,128)S(1)}, f32[6,16,512]{2,1,0:T(8,128)S(1)}, u32[]{:S(2)}, u32[]{:S(2)}) %collective-permute-start.9) | collective-permute-done | bytes 196640 | tf_op jit(solution)/shard_map/ppermute | solution.py:378
  50.4 2.5 %settle.13 = (f32[16,8,2048]{2,1,0:T(8,128)}, bf16[256,128]{1,0:T(8,128)(2,1)S(1)}, f32[128,128]{1,0:T(8,128)S(1)}) custom-call(s32[5]{0:T(128)S(1)} %convert_element_type.17.side.refs_0_, f32[6,16,512]{2,1,0:T(8,128)S(1)} %collective-permute-done.9.refs_1_, f32[2,16,512]{2,1,0:T(8,128)S(1)} %get-tuple-element.59.refs_2_, ...), custom_call_target="tpu_custom_call", output_to_operand_aliasing={{0}: (13, {})} | custom-call | flops 4000000000 | tf_op jit(solution)/shard_map/settle/pallas_call | solution.py:315
  52.9 0.8 %collective-permute-done.8.refs_1_ = f32[6,16,512]{2,1,0:T(8,128)S(1)} collective-permute-done((f32[6,16,512]{2,1,0:T(8,128)S(1)}, f32[6,16,512]{2,1,0:T(8,128)S(1)}, u32[]{:S(2)}, u32[]{:S(2)}) %collective-permute-start.8) | collective-permute-done | bytes 196640 | tf_op jit(solution)/shard_map/ppermute | solution.py:378
  53.7 2.5 %settle.14 = (f32[16,8,2048]{2,1,0:T(8,128)}, bf16[256,128]{1,0:T(8,128)(2,1)S(1)}, f32[128,128]{1,0:T(8,128)S(1)}) custom-call(s32[5]{0:T(128)S(1)} %convert_element_type.17.side.refs_0_, f32[6,16,512]{2,1,0:T(8,128)S(1)} %collective-permute-done.8.refs_1_, f32[2,16,512]{2,1,0:T(8,128)S(1)} %get-tuple-element.57.refs_2_, ...), custom_call_target="tpu_custom_call", output_to_operand_aliasing={{0}: (13, {})} | custom-call | flops 4000000000 | tf_op jit(solution)/shard_map/settle/pallas_call | solution.py:315
  56.2 0.1 collective-permute-done.7.refs_1_
  56.3 3.0 %settle.15 = f32[16,8,2048]{2,1,0:T(8,128)} custom-call(s32[5]{0:T(128)S(1)} %convert_element_type.17.side.refs_0_, f32[6,16,640]{2,1,0:T(8,128)S(1)} %collective-permute-done.7.refs_1_, f32[2,16,640]{2,1,0:T(8,128)S(1)} %get-tuple-element.55.refs_2_, f32[6,16,640]{2,1,0:T(8,128)S(1)} %get-tuple-element.54.refs_3_, ...), custom_call_target="tpu_custom_call", output_to_operand_aliasing={{}: (13, {})} | custom-call | flops 4000000000 | tf_op jit(solution)/shard_map/settle/pallas_call | solution.py:315
  (19 shorter events, 0.1 us)
Async XLA Ops:
  0.0 1.2 %copy-start = (f32[16,8,2048]{2,1,0:T(8,128)S(1)}, f32[16,8,2048]{2,1,0:T(8,128)}, u32[]{:S(2)}) copy-start(f32[16,8,2048]{2,1,0:T(8,128)} %own.9) | copy-start | bytes 3145732
  1.2 6.1 %copy-start.1 = (f32[16,8,2048]{2,1,0:T(8,128)S(1)}, f32[16,8,2048]{2,1,0:T(8,128)}, u32[]{:S(2)}) copy-start(f32[16,8,2048]{2,1,0:T(8,128)} %own.9) | copy-start | bytes 3145732
  1.8 26.4 %collective-permute-start = (f32[6,8,2048]{2,1,0:T(8,128)S(1)}, f32[6,8,2048]{2,1,0:T(8,128)S(1)}, u32[]{:S(2)}, u32[]{:S(2)}) collective-permute-start(f32[6,8,2048]{2,1,0:T(8,128)S(1)} %get-tuple-element.38.refs_1_), channel_id=1, source_target_pairs={{0,7},{1,0},{2,1},{3,2},{4,3},{5,4},{6,5},{7,6},{8,15},{9,8},{10,9... | collective-permute-start | bytes 1179656 | tf_op jit(solution)/shard_map/ppermute | solution.py:358
  6.5 0.7 %copy-start.5 = (f32[8,16]{1,0:T(8,128)S(1)}, f32[8,16]{1,0:T(8,128)}, u32[]{:S(2)}) copy-start(f32[8,16]{1,0:T(8,128)} %param.6) | copy-start | bytes 1540
  7.5 6.8 %collective-permute-start.1 = (f32[6,8,2176]{2,1,0:T(8,128)S(1)}, f32[6,8,2176]{2,1,0:T(8,128)S(1)}, u32[]{:S(2)}, u32[]{:S(2)}) collective-permute-start(f32[6,8,2176]{2,1,0:T(8,128)S(1)} %pad_maximum_fusion), channel_id=1, source_target_pairs={{0,8},{8,0},{16,24},{24,16},{32,40},{40,32},{48,56},{56,48},{64,72... | collective-permute-start | bytes 1253384 | tf_op jit(solution)/shard_map/ppermute | solution.py:355
  8.5 4.9 %copy-start.3 = (f32[8,2048]{1,0:T(8,128)S(1)}, f32[8,2048]{1,0:T(8,128)}, u32[]{:S(2)}) copy-start(f32[8,2048]{1,0:T(8,128)} %param.8) | copy-start | bytes 196612
  9.3 13.2 %collective-permute-start.2 = (f32[6,8,2176]{2,1,0:T(8,128)}, f32[6,8,2176]{2,1,0:T(8,128)S(1)}, u32[]{:S(2)}, u32[]{:S(2)}) collective-permute-start(f32[6,8,2176]{2,1,0:T(8,128)} %pad_maximum_fusion.1), channel_id=1, source_target_pairs={{8,16},{16,8},{24,32},{32,24},{40,48},{48,40},{56,64},{64,56},{72,... | collective-permute-start | bytes 1253384 | tf_op jit(solution)/shard_map/ppermute | solution.py:354
  13.4 0.8 %copy-start.4 = (s32[8,2048]{1,0:T(8,128)S(1)}, s32[8,2048]{1,0:T(8,128)}, u32[]{:S(2)}) copy-start(s32[8,2048]{1,0:T(8,128)} %param.7) | copy-start | bytes 196612
  23.5 7.1 %collective-permute-start.6 = (f32[6,16,512]{2,1,0:T(8,128)S(1)}, f32[6,16,512]{2,1,0:T(8,128)S(1)}, u32[]{:S(2)}, u32[]{:S(2)}) collective-permute-start(f32[6,16,512]{2,1,0:T(8,128)S(1)} %get-tuple-element.46.refs_4_), channel_id=1, source_target_pairs={{0,7},{1,0},{2,1},{3,2},{4,3},{5,4},{6,5},{7,6},{8,15},{9,8},{10,9... | collective-permute-start | bytes 589832 | tf_op jit(solution)/shard_map/ppermute | solution.py:360
  24.5 10.3 %collective-permute-start.5 = (f32[6,16,512]{2,1,0:T(8,128)S(1)}, f32[6,16,512]{2,1,0:T(8,128)S(1)}, u32[]{:S(2)}, u32[]{:S(2)}) collective-permute-start(f32[6,16,512]{2,1,0:T(8,128)S(1)} %get-tuple-element.44.refs_4_), channel_id=1, source_target_pairs={{0,7},{1,0},{2,1},{3,2},{4,3},{5,4},{6,5},{7,6},{8,15},{9,8},{10,9... | collective-permute-start | bytes 589832 | tf_op jit(solution)/shard_map/ppermute | solution.py:360
  26.3 12.6 %collective-permute-start.4 = (f32[6,16,512]{2,1,0:T(8,128)S(1)}, f32[6,16,512]{2,1,0:T(8,128)S(1)}, u32[]{:S(2)}, u32[]{:S(2)}) collective-permute-start(f32[6,16,512]{2,1,0:T(8,128)S(1)} %get-tuple-element.42.refs_4_), channel_id=1, source_target_pairs={{0,7},{1,0},{2,1},{3,2},{4,3},{5,4},{6,5},{7,6},{8,15},{9,8},{10,9... | collective-permute-start | bytes 589832 | tf_op jit(solution)/shard_map/ppermute | solution.py:360
  27.3 15.8 %collective-permute-start.3 = (f32[6,16,512]{2,1,0:T(8,128)S(1)}, f32[6,16,512]{2,1,0:T(8,128)S(1)}, u32[]{:S(2)}, u32[]{:S(2)}) collective-permute-start(f32[6,16,512]{2,1,0:T(8,128)S(1)} %get-tuple-element.40.refs_4_), channel_id=1, source_target_pairs={{0,7},{1,0},{2,1},{3,2},{4,3},{5,4},{6,5},{7,6},{8,15},{9,8},{10,9... | collective-permute-start | bytes 589832 | tf_op jit(solution)/shard_map/ppermute | solution.py:360
  30.5 0.7 %copy-start.2 = (f32[2048]{0:T(1024)S(1)}, f32[2048]{0:T(1024)}, u32[]{:S(2)}) copy-start(f32[2048]{0:T(1024)} %param.9) | copy-start | bytes 24580
  33.3 12.9 %collective-permute-start.10 = (f32[6,16,384]{2,1,0:T(8,128)S(1)}, f32[6,16,384]{2,1,0:T(8,128)S(1)}, u32[]{:S(2)}, u32[]{:S(2)}) collective-permute-start(f32[6,16,384]{2,1,0:T(8,128)S(1)} %get-tuple-element.60.refs_3_), channel_id=1, source_target_pairs={{0,1},{1,2},{2,3},{3,4},{4,5},{5,6},{6,7},{7,0},{8,9},{9,10},{10,1... | collective-permute-start | bytes 442376 | tf_op jit(solution)/shard_map/ppermute | solution.py:378
  37.2 13.2 %collective-permute-start.9 = (f32[6,16,512]{2,1,0:T(8,128)S(1)}, f32[6,16,512]{2,1,0:T(8,128)S(1)}, u32[]{:S(2)}, u32[]{:S(2)}) collective-permute-start(f32[6,16,512]{2,1,0:T(8,128)S(1)} %get-tuple-element.58.refs_3_), channel_id=1, source_target_pairs={{0,1},{1,2},{2,3},{3,4},{4,5},{5,6},{6,7},{7,0},{8,9},{9,10},{10,1... | collective-permute-start | bytes 589832 | tf_op jit(solution)/shard_map/ppermute | solution.py:378
  41.4 12.3 %collective-permute-start.8 = (f32[6,16,512]{2,1,0:T(8,128)S(1)}, f32[6,16,512]{2,1,0:T(8,128)S(1)}, u32[]{:S(2)}, u32[]{:S(2)}) collective-permute-start(f32[6,16,512]{2,1,0:T(8,128)S(1)} %get-tuple-element.56.refs_3_), channel_id=1, source_target_pairs={{0,1},{1,2},{2,3},{3,4},{4,5},{5,6},{6,7},{7,0},{8,9},{9,10},{10,1... | collective-permute-start | bytes 589832 | tf_op jit(solution)/shard_map/ppermute | solution.py:378
  45.9 10.4 %collective-permute-start.7 = (f32[6,16,640]{2,1,0:T(8,128)S(1)}, f32[6,16,640]{2,1,0:T(8,128)S(1)}, u32[]{:S(2)}, u32[]{:S(2)}) collective-permute-start(f32[6,16,640]{2,1,0:T(8,128)S(1)} %get-tuple-element.54.refs_3_), channel_id=1, source_target_pairs={{0,1},{1,2},{2,3},{3,4},{4,5},{5,6},{6,7},{7,0},{8,9},{9,10},{10,1... | collective-permute-start | bytes 737288 | tf_op jit(solution)/shard_map/ppermute | solution.py:378

commit v3 on v2

--- a/solution.py
+++ b/solution.py
@@ -84,7 +84,7 @@
         sent[:, :, at] = turned[:WIDE]
         kept[:, :, at] = turned[WIDE:]
 
-    repeat(own.shape[-1] // LANES, 2, body)
+    repeat(own.shape[-1] // LANES, 4, body)
 
 
 def outer_kernel(side, own, near, far, sent, kept):
@@ -105,7 +105,7 @@
         sent[:, :, at] = turned[:WIDE]
         kept[:, :, at] = turned[WIDE:]
 
-    repeat(own.shape[-1] // LANES, 2, body)
+    repeat(own.shape[-1] // LANES, 4, body)
 
 
 def block(array_or_shape, width, index):

time: 59.8 us -> 59.7 us (level)
  no operation moved by 1% of the time
where the time goes in v3:
time: 59.7 us; the launch traced here: 59.4 us
  Pallas kernels  22.9 us (38%)
  waiting for transfers between devices  18.3 us (31%)
  starting transfers between devices  12.8 us (21%)
  local copies, waits for them, and re-layouts  3.97 us (7%)
  other arithmetic  1.04 us (2%)
    pallas_call x8, Pallas kernels, settle(): pl.pallas_call(functools.partial(settle_kernel, plan), grid=(1,), out_sha...  19.8 us
    ppermute x1, waiting for transfers between devices, on_device(): far = lax.ppermute(far, 'vol', across)  8.22 us
    ppermute x4, waiting for transfers between devices, on_device(): outer = [(*o, lax.ppermute(o[0], 'rate', rate_back)) for o in outer]  7.09 us
    ppermute x1, starting transfers between devices, on_device(): inner = (*inner, lax.ppermute(inner[0], 'rate', rate_back))  4.75 us
    ppermute x1, starting transfers between devices, on_device(): far = lax.ppermute(far, 'vol', across)  3.91 us
    unnamed x12, local copies, waits for them, and re-layouts  3.34 us
    ppermute x4, waiting for transfers between devices, on_device(): onward.append((lax.ppermute(pieces[1], 'rate', rate_on), *pieces))  3.01 us
    pallas_call x4, Pallas kernels, smooth_outer(): pl.pallas_call(outer_kernel, grid=(1,), out_shape=outs, in_specs=[SMEM] +...  2.68 us
  transfers between devices with their start and end apart: 11, of which 8 were waited for; matrix products, arithmetic and copies ran while one was open for 3% of the time, Pallas kernels for 33%

profile of v3, /device:TPU:25, one launch (start us, length us, event | category | flops | bytes accessed | tf_op | source)
XLA Modules:
  0.0 59.4 jit_solution(8355021668209923392)
XLA Ops:
  0.0 1.2 %copy-done = f32[16,8,2048]{2,1,0:T(8,128)S(1)} copy-done((f32[16,8,2048]{2,1,0:T(8,128)S(1)}, f32[16,8,2048]{2,1,0:T(8,128)}, u32[]{:S(2)}) %copy-start) | copy-done | bytes 1048600
  1.2 0.5 smooth_inner.1
  1.7 4.8 %collective-permute-start = (f32[6,8,2048]{2,1,0:T(8,128)S(1)}, f32[6,8,2048]{2,1,0:T(8,128)S(1)}, u32[]{:S(2)}, u32[]{:S(2)}) collective-permute-start(f32[6,8,2048]{2,1,0:T(8,128)S(1)} %get-tuple-element.38.refs_1_), channel_id=1, source_target_pairs={{0,7},{1,0},{2,1},{3,2},{4,3},{5,4},{6,5},{7,6},{8,15},{9,8},{10,9... | collective-permute-start | bytes 1179656 | tf_op jit(solution)/shard_map/ppermute | solution.py:358
  6.5 0.7 %copy-done.5 = f32[8,16]{1,0:T(8,128)S(1)} copy-done((f32[8,16]{1,0:T(8,128)S(1)}, f32[8,16]{1,0:T(8,128)}, u32[]{:S(2)}) %copy-start.5) | copy-done | bytes 536
  7.1 0.1 copy.12
  7.3 0.1 constant_dynamic-slice_fusion
  7.4 1.0 %collective-permute-start.1 = (f32[6,8,2176]{2,1,0:T(8,128)S(1)}, f32[6,8,2176]{2,1,0:T(8,128)S(1)}, u32[]{:S(2)}, u32[]{:S(2)}) collective-permute-start(f32[6,8,2176]{2,1,0:T(8,128)S(1)} %pad_maximum_fusion), channel_id=1, source_target_pairs={{0,8},{8,0},{16,24},{24,16},{32,40},{40,32},{48,56},{56,48},{64,72... | collective-permute-start | bytes 1253384 | tf_op jit(solution)/shard_map/ppermute | solution.py:355
  8.4 0.8 %pad_maximum_fusion.1 = f32[6,8,2176]{2,1,0:T(8,128)} fusion(f32[6,8,128]{2,1,0:T(8,128)S(1)} %get-tuple-element.79, f32[6,8,2048]{2,1,0:T(8,128)S(1)} %get-tuple-element.73), kind=kLoop, calls=%fused_computation.1 | loop fusion | flops 104448 | bytes 835584 | tf_op jit(solution)/shard_map/concatenate | solution.py:351
  9.2 3.9 %collective-permute-start.2 = (f32[6,8,2176]{2,1,0:T(8,128)}, f32[6,8,2176]{2,1,0:T(8,128)S(1)}, u32[]{:S(2)}, u32[]{:S(2)}) collective-permute-start(f32[6,8,2176]{2,1,0:T(8,128)} %pad_maximum_fusion.1), channel_id=1, source_target_pairs={{8,16},{16,8},{24,32},{32,24},{40,48},{48,40},{56,64},{64,56},{72,... | collective-permute-start | bytes 1253384 | tf_op jit(solution)/shard_map/ppermute | solution.py:354
  13.2 0.1 stack.23
  13.4 0.8 %copy-done.4 = s32[8,2048]{1,0:T(8,128)S(1)} copy-done((s32[8,2048]{1,0:T(8,128)S(1)}, s32[8,2048]{1,0:T(8,128)}, u32[]{:S(2)}) %copy-start.4) | copy-done | bytes 65560
  14.2 0.0 collective-permute-done.1.near
  14.2 8.2 %collective-permute-done.2.far = f32[6,8,2176]{2,1,0:T(8,128)S(1)} collective-permute-done((f32[6,8,2176]{2,1,0:T(8,128)}, f32[6,8,2176]{2,1,0:T(8,128)S(1)}, u32[]{:S(2)}, u32[]{:S(2)}) %collective-permute-start.2) | collective-permute-done | bytes 417824 | tf_op jit(solution)/shard_map/ppermute | solution.py:354
  22.4 0.1 select_reduce_fusion.1
  22.5 0.1 copy.14
  22.6 0.1 copy.13
  22.7 0.7 %smooth_outer.7 = (f32[6,16,512]{2,1,0:T(8,128)S(1)}, f32[2,16,512]{2,1,0:T(8,128)S(1)}) custom-call(s32[5]{0:T(128)S(1)} %convert_element_type.17.side.refs_0_, f32[16,8,2048]{2,1,0:T(8,128)S(1)} %copy-done.1, f32[6,8,2176]{2,1,0:T(8,128)S(1)} %collective-permute-done.1.near, f32[6,8,2176]{2,1,0:T(8,128)S(1)} %collective-permute-done.2.far), custom_call_target="tpu_custom_call" | custom-call | flops 1000000000 | tf_op jit(solution)/shard_map/smooth_outer/pallas_call | solution.py:136
  23.4 0.3 collective-permute-start.6
  23.7 0.7 %smooth_outer.6 = (f32[6,16,512]{2,1,0:T(8,128)S(1)}, f32[2,16,512]{2,1,0:T(8,128)S(1)}) custom-call(s32[5]{0:T(128)S(1)} %convert_element_type.17.side.refs_0_, f32[16,8,2048]{2,1,0:T(8,128)S(1)} %copy-done.1, f32[6,8,2176]{2,1,0:T(8,128)S(1)} %collective-permute-done.1.near, f32[6,8,2176]{2,1,0:T(8,128)S(1)} %collective-permute-done.2.far), custom_call_target="tpu_custom_call" | custom-call | flops 1000000000 | tf_op jit(solution)/shard_map/smooth_outer/pallas_call | solution.py:136
  24.3 1.1 %collective-permute-start.5 = (f32[6,16,512]{2,1,0:T(8,128)S(1)}, f32[6,16,512]{2,1,0:T(8,128)S(1)}, u32[]{:S(2)}, u32[]{:S(2)}) collective-permute-start(f32[6,16,512]{2,1,0:T(8,128)S(1)} %get-tuple-element.44.refs_4_), channel_id=1, source_target_pairs={{0,7},{1,0},{2,1},{3,2},{4,3},{5,4},{6,5},{7,6},{8,15},{9,8},{10,9... | collective-permute-start | bytes 589832 | tf_op jit(solution)/shard_map/ppermute | solution.py:360
  25.5 0.7 %smooth_outer.5 = (f32[6,16,512]{2,1,0:T(8,128)S(1)}, f32[2,16,512]{2,1,0:T(8,128)S(1)}) custom-call(s32[5]{0:T(128)S(1)} %convert_element_type.17.side.refs_0_, f32[16,8,2048]{2,1,0:T(8,128)S(1)} %copy-done.1, f32[6,8,2176]{2,1,0:T(8,128)S(1)} %collective-permute-done.1.near, f32[6,8,2176]{2,1,0:T(8,128)S(1)} %collective-permute-done.2.far), custom_call_target="tpu_custom_call" | custom-call | flops 1000000000 | tf_op jit(solution)/shard_map/smooth_outer/pallas_call | solution.py:136
  26.2 0.3 collective-permute-start.4
  26.5 0.7 %smooth_outer.4 = (f32[6,16,512]{2,1,0:T(8,128)S(1)}, f32[2,16,512]{2,1,0:T(8,128)S(1)}) custom-call(s32[5]{0:T(128)S(1)} %convert_element_type.17.side.refs_0_, f32[16,8,2048]{2,1,0:T(8,128)S(1)} %copy-done.1, f32[6,8,2176]{2,1,0:T(8,128)S(1)} %collective-permute-done.1.near, f32[6,8,2176]{2,1,0:T(8,128)S(1)} %collective-permute-done.2.far), custom_call_target="tpu_custom_call" | custom-call | flops 1000000000 | tf_op jit(solution)/shard_map/smooth_outer/pallas_call | solution.py:136
  27.1 0.8 %collective-permute-start.3 = (f32[6,16,512]{2,1,0:T(8,128)S(1)}, f32[6,16,512]{2,1,0:T(8,128)S(1)}, u32[]{:S(2)}, u32[]{:S(2)}) collective-permute-start(f32[6,16,512]{2,1,0:T(8,128)S(1)} %get-tuple-element.40.refs_4_), channel_id=1, source_target_pairs={{0,7},{1,0},{2,1},{3,2},{4,3},{5,4},{6,5},{7,6},{8,15},{9,8},{10,9... | collective-permute-start | bytes 589832 | tf_op jit(solution)/shard_map/ppermute | solution.py:360
  28.0 0.1 fusion.5
  28.1 0.0 collective-permute-done.refs_3_
  28.1 2.3 %collective-permute-done.6.refs_6_ = f32[6,16,512]{2,1,0:T(8,128)S(1)} collective-permute-done((f32[6,16,512]{2,1,0:T(8,128)S(1)}, f32[6,16,512]{2,1,0:T(8,128)S(1)}, u32[]{:S(2)}, u32[]{:S(2)}) %collective-permute-start.6) | collective-permute-done | bytes 196640 | tf_op jit(solution)/shard_map/ppermute | solution.py:360
  30.4 0.1 broadcast_in_dim.9.refs_12_
  30.5 0.6 %copy-done.2 = f32[2048]{0:T(1024)S(1)} copy-done((f32[2048]{0:T(1024)S(1)}, f32[2048]{0:T(1024)}, u32[]{:S(2)}) %copy-start.2) | copy-done | bytes 8216
  31.1 2.1 %settle.8 = (f32[2,16,384]{2,1,0:T(8,128)S(1)}, f32[6,16,384]{2,1,0:T(8,128)S(1)}, bf16[384,128]{1,0:T(8,128)(2,1)S(1)}, f32[192,128]{1,0:T(8,128)S(1)}) custom-call(s32[5]{0:T(128)S(1)} %convert_element_type.17.side.refs_0_, f32[6,8,2048]{2,1,0:T(8,128)S(1)} %get-tuple-element.38.refs_1_, f32[2,8,2048]{2,1,0:T(8,128)S(1)} %get-tuple-element.39.refs_2_, ...), custom_call_target="tpu_custom_call" | custom-call | flops 4000000000 | tf_op jit(solution)/shard_map/settle/pallas_call | solution.py:315
  33.2 0.1 collective-permute-start.10
  33.3 1.3 %collective-permute-done.5.refs_6_ = f32[6,16,512]{2,1,0:T(8,128)S(1)} collective-permute-done((f32[6,16,512]{2,1,0:T(8,128)S(1)}, f32[6,16,512]{2,1,0:T(8,128)S(1)}, u32[]{:S(2)}, u32[]{:S(2)}) %collective-permute-start.5) | collective-permute-done | bytes 196640 | tf_op jit(solution)/shard_map/ppermute | solution.py:360
  34.6 2.4 %settle.9 = (f32[2,16,512]{2,1,0:T(8,128)S(1)}, f32[6,16,512]{2,1,0:T(8,128)S(1)}, bf16[384,128]{1,0:T(8,128)(2,1)S(1)}, f32[192,128]{1,0:T(8,128)S(1)}) custom-call(s32[5]{0:T(128)S(1)} %convert_element_type.17.side.refs_0_, f32[6,8,2048]{2,1,0:T(8,128)S(1)} %get-tuple-element.38.refs_1_, f32[2,8,2048]{2,1,0:T(8,128)S(1)} %get-tuple-element.39.refs_2_, ...), custom_call_target="tpu_custom_call" | custom-call | flops 4000000000 | tf_op jit(solution)/shard_map/settle/pallas_call | solution.py:315
  37.1 0.1 collective-permute-start.9
  37.2 1.7 %collective-permute-done.4.refs_6_ = f32[6,16,512]{2,1,0:T(8,128)S(1)} collective-permute-done((f32[6,16,512]{2,1,0:T(8,128)S(1)}, f32[6,16,512]{2,1,0:T(8,128)S(1)}, u32[]{:S(2)}, u32[]{:S(2)}) %collective-permute-start.4) | collective-permute-done | bytes 196640 | tf_op jit(solution)/shard_map/ppermute | solution.py:360
  38.8 2.4 %settle.10 = (f32[2,16,512]{2,1,0:T(8,128)S(1)}, f32[6,16,512]{2,1,0:T(8,128)S(1)}, bf16[384,128]{1,0:T(8,128)(2,1)S(1)}, f32[192,128]{1,0:T(8,128)S(1)}) custom-call(s32[5]{0:T(128)S(1)} %convert_element_type.17.side.refs_0_, f32[6,8,2048]{2,1,0:T(8,128)S(1)} %get-tuple-element.38.refs_1_, f32[2,8,2048]{2,1,0:T(8,128)S(1)} %get-tuple-element.39.refs_2_, ...), custom_call_target="tpu_custom_call" | custom-call | flops 4000000000 | tf_op jit(solution)/shard_map/settle/pallas_call | solution.py:315
  41.3 0.1 collective-permute-start.8
  41.4 1.7 %collective-permute-done.3.refs_6_ = f32[6,16,512]{2,1,0:T(8,128)S(1)} collective-permute-done((f32[6,16,512]{2,1,0:T(8,128)S(1)}, f32[6,16,512]{2,1,0:T(8,128)S(1)}, u32[]{:S(2)}, u32[]{:S(2)}) %collective-permute-start.3) | collective-permute-done | bytes 196640 | tf_op jit(solution)/shard_map/ppermute | solution.py:360
  43.1 2.8 %settle.11 = (f32[2,16,640]{2,1,0:T(8,128)S(1)}, f32[6,16,640]{2,1,0:T(8,128)S(1)}) custom-call(s32[5]{0:T(128)S(1)} %convert_element_type.17.side.refs_0_, f32[6,8,2048]{2,1,0:T(8,128)S(1)} %get-tuple-element.38.refs_1_, f32[2,8,2048]{2,1,0:T(8,128)S(1)} %get-tuple-element.39.refs_2_, f32[6,8,2048]{2,1,0:T(8,128)S(1)} %collective-permute-done.refs_3_, ...), custom_call_target="tpu_custom_call" | custom-call | flops 4000000000 | tf_op jit(solution)/shard_map/settle/pallas_call | solution.py:315
  45.9 0.3 collective-permute-start.7
  46.1 0.1 broadcast_in_dim.21.refs_9_
  46.2 2.0 %settle.12 = (f32[16,8,2048]{2,1,0:T(8,128)}, bf16[256,128]{1,0:T(8,128)(2,1)S(1)}, f32[128,128]{1,0:T(8,128)S(1)}) custom-call(s32[5]{0:T(128)S(1)} %convert_element_type.17.side.refs_0_, f32[6,16,384]{2,1,0:T(8,128)S(1)} %collective-permute-done.10.refs_1_, f32[2,16,384]{2,1,0:T(8,128)S(1)} %get-tuple-element.61.refs_2_, ...), custom_call_target="tpu_custom_call" | custom-call | flops 4000000000 | tf_op jit(solution)/shard_map/settle/pallas_call | solution.py:315
  48.2 2.1 %collective-permute-done.9.refs_1_ = f32[6,16,512]{2,1,0:T(8,128)S(1)} collective-permute-done((f32[6,16,512]{2,1,0:T(8,128)S(1)}, f32[6,16,512]{2,1,0:T(8,128)S(1)}, u32[]{:S(2)}, u32[]{:S(2)}) %collective-permute-start.9) | collective-permute-done | bytes 196640 | tf_op jit(solution)/shard_map/ppermute | solution.py:378
  50.3 2.5 %settle.13 = (f32[16,8,2048]{2,1,0:T(8,128)}, bf16[256,128]{1,0:T(8,128)(2,1)S(1)}, f32[128,128]{1,0:T(8,128)S(1)}) custom-call(s32[5]{0:T(128)S(1)} %convert_element_type.17.side.refs_0_, f32[6,16,512]{2,1,0:T(8,128)S(1)} %collective-permute-done.9.refs_1_, f32[2,16,512]{2,1,0:T(8,128)S(1)} %get-tuple-element.59.refs_2_, ...), custom_call_target="tpu_custom_call", output_to_operand_aliasing={{0}: (13, {})} | custom-call | flops 4000000000 | tf_op jit(solution)/shard_map/settle/pallas_call | solution.py:315
  52.8 0.8 %collective-permute-done.8.refs_1_ = f32[6,16,512]{2,1,0:T(8,128)S(1)} collective-permute-done((f32[6,16,512]{2,1,0:T(8,128)S(1)}, f32[6,16,512]{2,1,0:T(8,128)S(1)}, u32[]{:S(2)}, u32[]{:S(2)}) %collective-permute-start.8) | collective-permute-done | bytes 196640 | tf_op jit(solution)/shard_map/ppermute | solution.py:378
  53.6 2.5 %settle.14 = (f32[16,8,2048]{2,1,0:T(8,128)}, bf16[256,128]{1,0:T(8,128)(2,1)S(1)}, f32[128,128]{1,0:T(8,128)S(1)}) custom-call(s32[5]{0:T(128)S(1)} %convert_element_type.17.side.refs_0_, f32[6,16,512]{2,1,0:T(8,128)S(1)} %collective-permute-done.8.refs_1_, f32[2,16,512]{2,1,0:T(8,128)S(1)} %get-tuple-element.57.refs_2_, ...), custom_call_target="tpu_custom_call", output_to_operand_aliasing={{0}: (13, {})} | custom-call | flops 4000000000 | tf_op jit(solution)/shard_map/settle/pallas_call | solution.py:315
  56.1 0.1 collective-permute-done.7.refs_1_
  56.2 3.0 %settle.15 = f32[16,8,2048]{2,1,0:T(8,128)} custom-call(s32[5]{0:T(128)S(1)} %convert_element_type.17.side.refs_0_, f32[6,16,640]{2,1,0:T(8,128)S(1)} %collective-permute-done.7.refs_1_, f32[2,16,640]{2,1,0:T(8,128)S(1)} %get-tuple-element.55.refs_2_, f32[6,16,640]{2,1,0:T(8,128)S(1)} %get-tuple-element.54.refs_3_, ...), custom_call_target="tpu_custom_call", output_to_operand_aliasing={{}: (13, {})} | custom-call | flops 4000000000 | tf_op jit(solution)/shard_map/settle/pallas_call | solution.py:315
  (19 shorter events, 0.1 us)
Async XLA Ops:
  0.0 1.2 %copy-start = (f32[16,8,2048]{2,1,0:T(8,128)S(1)}, f32[16,8,2048]{2,1,0:T(8,128)}, u32[]{:S(2)}) copy-start(f32[16,8,2048]{2,1,0:T(8,128)} %own.9) | copy-start | bytes 3145732
  1.2 6.1 %copy-start.1 = (f32[16,8,2048]{2,1,0:T(8,128)S(1)}, f32[16,8,2048]{2,1,0:T(8,128)}, u32[]{:S(2)}) copy-start(f32[16,8,2048]{2,1,0:T(8,128)} %own.9) | copy-start | bytes 3145732
  1.7 26.4 %collective-permute-start = (f32[6,8,2048]{2,1,0:T(8,128)S(1)}, f32[6,8,2048]{2,1,0:T(8,128)S(1)}, u32[]{:S(2)}, u32[]{:S(2)}) collective-permute-start(f32[6,8,2048]{2,1,0:T(8,128)S(1)} %get-tuple-element.38.refs_1_), channel_id=1, source_target_pairs={{0,7},{1,0},{2,1},{3,2},{4,3},{5,4},{6,5},{7,6},{8,15},{9,8},{10,9... | collective-permute-start | bytes 1179656 | tf_op jit(solution)/shard_map/ppermute | solution.py:358
  6.5 0.7 %copy-start.5 = (f32[8,16]{1,0:T(8,128)S(1)}, f32[8,16]{1,0:T(8,128)}, u32[]{:S(2)}) copy-start(f32[8,16]{1,0:T(8,128)} %param.6) | copy-start | bytes 1540
  7.4 6.8 %collective-permute-start.1 = (f32[6,8,2176]{2,1,0:T(8,128)S(1)}, f32[6,8,2176]{2,1,0:T(8,128)S(1)}, u32[]{:S(2)}, u32[]{:S(2)}) collective-permute-start(f32[6,8,2176]{2,1,0:T(8,128)S(1)} %pad_maximum_fusion), channel_id=1, source_target_pairs={{0,8},{8,0},{16,24},{24,16},{32,40},{40,32},{48,56},{56,48},{64,72... | collective-permute-start | bytes 1253384 | tf_op jit(solution)/shard_map/ppermute | solution.py:355
  8.4 4.9 %copy-start.3 = (f32[8,2048]{1,0:T(8,128)S(1)}, f32[8,2048]{1,0:T(8,128)}, u32[]{:S(2)}) copy-start(f32[8,2048]{1,0:T(8,128)} %param.8) | copy-start | bytes 196612
  9.2 13.2 %collective-permute-start.2 = (f32[6,8,2176]{2,1,0:T(8,128)}, f32[6,8,2176]{2,1,0:T(8,128)S(1)}, u32[]{:S(2)}, u32[]{:S(2)}) collective-permute-start(f32[6,8,2176]{2,1,0:T(8,128)} %pad_maximum_fusion.1), channel_id=1, source_target_pairs={{8,16},{16,8},{24,32},{32,24},{40,48},{48,40},{56,64},{64,56},{72,... | collective-permute-start | bytes 1253384 | tf_op jit(solution)/shard_map/ppermute | solution.py:354
  13.3 0.8 %copy-start.4 = (s32[8,2048]{1,0:T(8,128)S(1)}, s32[8,2048]{1,0:T(8,128)}, u32[]{:S(2)}) copy-start(s32[8,2048]{1,0:T(8,128)} %param.7) | copy-start | bytes 196612
  23.4 7.1 %collective-permute-start.6 = (f32[6,16,512]{2,1,0:T(8,128)S(1)}, f32[6,16,512]{2,1,0:T(8,128)S(1)}, u32[]{:S(2)}, u32[]{:S(2)}) collective-permute-start(f32[6,16,512]{2,1,0:T(8,128)S(1)} %get-tuple-element.46.refs_4_), channel_id=1, source_target_pairs={{0,7},{1,0},{2,1},{3,2},{4,3},{5,4},{6,5},{7,6},{8,15},{9,8},{10,9... | collective-permute-start | bytes 589832 | tf_op jit(solution)/shard_map/ppermute | solution.py:360
  24.3 10.3 %collective-permute-start.5 = (f32[6,16,512]{2,1,0:T(8,128)S(1)}, f32[6,16,512]{2,1,0:T(8,128)S(1)}, u32[]{:S(2)}, u32[]{:S(2)}) collective-permute-start(f32[6,16,512]{2,1,0:T(8,128)S(1)} %get-tuple-element.44.refs_4_), channel_id=1, source_target_pairs={{0,7},{1,0},{2,1},{3,2},{4,3},{5,4},{6,5},{7,6},{8,15},{9,8},{10,9... | collective-permute-start | bytes 589832 | tf_op jit(solution)/shard_map/ppermute | solution.py:360
  26.2 12.7 %collective-permute-start.4 = (f32[6,16,512]{2,1,0:T(8,128)S(1)}, f32[6,16,512]{2,1,0:T(8,128)S(1)}, u32[]{:S(2)}, u32[]{:S(2)}) collective-permute-start(f32[6,16,512]{2,1,0:T(8,128)S(1)} %get-tuple-element.42.refs_4_), channel_id=1, source_target_pairs={{0,7},{1,0},{2,1},{3,2},{4,3},{5,4},{6,5},{7,6},{8,15},{9,8},{10,9... | collective-permute-start | bytes 589832 | tf_op jit(solution)/shard_map/ppermute | solution.py:360
  27.1 15.9 %collective-permute-start.3 = (f32[6,16,512]{2,1,0:T(8,128)S(1)}, f32[6,16,512]{2,1,0:T(8,128)S(1)}, u32[]{:S(2)}, u32[]{:S(2)}) collective-permute-start(f32[6,16,512]{2,1,0:T(8,128)S(1)} %get-tuple-element.40.refs_4_), channel_id=1, source_target_pairs={{0,7},{1,0},{2,1},{3,2},{4,3},{5,4},{6,5},{7,6},{8,15},{9,8},{10,9... | collective-permute-start | bytes 589832 | tf_op jit(solution)/shard_map/ppermute | solution.py:360
  30.4 0.7 %copy-start.2 = (f32[2048]{0:T(1024)S(1)}, f32[2048]{0:T(1024)}, u32[]{:S(2)}) copy-start(f32[2048]{0:T(1024)} %param.9) | copy-start | bytes 24580
  33.2 12.9 %collective-permute-start.10 = (f32[6,16,384]{2,1,0:T(8,128)S(1)}, f32[6,16,384]{2,1,0:T(8,128)S(1)}, u32[]{:S(2)}, u32[]{:S(2)}) collective-permute-start(f32[6,16,384]{2,1,0:T(8,128)S(1)} %get-tuple-element.60.refs_3_), channel_id=1, source_target_pairs={{0,1},{1,2},{2,3},{3,4},{4,5},{5,6},{6,7},{7,0},{8,9},{9,10},{10,1... | collective-permute-start | bytes 442376 | tf_op jit(solution)/shard_map/ppermute | solution.py:378
  37.1 13.2 %collective-permute-start.9 = (f32[6,16,512]{2,1,0:T(8,128)S(1)}, f32[6,16,512]{2,1,0:T(8,128)S(1)}, u32[]{:S(2)}, u32[]{:S(2)}) collective-permute-start(f32[6,16,512]{2,1,0:T(8,128)S(1)} %get-tuple-element.58.refs_3_), channel_id=1, source_target_pairs={{0,1},{1,2},{2,3},{3,4},{4,5},{5,6},{6,7},{7,0},{8,9},{9,10},{10,1... | collective-permute-start | bytes 589832 | tf_op jit(solution)/shard_map/ppermute | solution.py:378
  41.3 12.3 %collective-permute-start.8 = (f32[6,16,512]{2,1,0:T(8,128)S(1)}, f32[6,16,512]{2,1,0:T(8,128)S(1)}, u32[]{:S(2)}, u32[]{:S(2)}) collective-permute-start(f32[6,16,512]{2,1,0:T(8,128)S(1)} %get-tuple-element.56.refs_3_), channel_id=1, source_target_pairs={{0,1},{1,2},{2,3},{3,4},{4,5},{5,6},{6,7},{7,0},{8,9},{9,10},{10,1... | collective-permute-start | bytes 589832 | tf_op jit(solution)/shard_map/ppermute | solution.py:378
  45.9 10.4 %collective-permute-start.7 = (f32[6,16,640]{2,1,0:T(8,128)S(1)}, f32[6,16,640]{2,1,0:T(8,128)S(1)}, u32[]{:S(2)}, u32[]{:S(2)}) collective-permute-start(f32[6,16,640]{2,1,0:T(8,128)S(1)} %get-tuple-element.54.refs_3_), channel_id=1, source_target_pairs={{0,1},{1,2},{2,3},{3,4},{4,5},{5,6},{6,7},{7,0},{8,9},{9,10},{10,1... | collective-permute-start | bytes 737288 | tf_op jit(solution)/shard_map/ppermute | solution.py:378

commit v4 on v3

--- a/solution.py
+++ b/solution.py
@@ -257,11 +257,21 @@
             outs[0][:, :, here] = onward[: rates - WIDE]
             outs[1][:, :, here] = onward[rates - WIDE :]
 
-    repeat(k_high - k_low, 4, choose)
+    count = k_high - k_low
+    half = count // 2 if whole else count
+    repeat(half, 4, choose)
     if whole:
-        copy = pltpu.make_async_copy(result, outs[0].at[:, :, pl.ds(k_low * LANES, (k_high - k_low) * LANES)], sem)
-        copy.start()
-        copy.wait()
+
+        def give(begin, length, which):
+            to = outs[0].at[:, :, pl.ds((k_low + begin) * LANES, length * LANES)]
+            return pltpu.make_async_copy(result.at[:, :, pl.ds(begin * LANES, length * LANES)], to, sem.at[which])
+
+        early, late = give(0, half, 0), give(half, count - half, 1)
+        early.start()
+        repeat(count - half, 4, lambda tile: choose(tile + half))
+        late.start()
+        early.wait()
+        late.wait()
 
 
 def cuts_of(section, index, tiles):
@@ -300,7 +310,7 @@
     if whole:
         outs = [jax.ShapeDtypeStruct((vols, rates, wealth), F32)]
         out_specs = [pl.BlockSpec(memory_space=pl.ANY)]
-        scratch += [pltpu.VMEM((vols, rates, count * LANES), F32), pltpu.SemaphoreType.DMA]
+        scratch += [pltpu.VMEM((vols, rates, count * LANES), F32), pltpu.SemaphoreType.DMA((2,))]
     else:
         outs = [jax.ShapeDtypeStruct((n, vols - EDGE, count * LANES), F32) for n in (rates - WIDE, WIDE)]
         out_specs = [full(o.shape) for o in outs]

time: 59.7 us -> 59.6 us (level)
  no operation moved by 1% of the time
where the time goes in v4:
time: 59.6 us; the launch traced here: 59.4 us
  Pallas kernels  22.8 us (38%)
  waiting for transfers between devices  18.4 us (31%)
  starting transfers between devices  12.8 us (21%)
  local copies, waits for them, and re-layouts  3.97 us (7%)
  other arithmetic  1.04 us (2%)
    pallas_call x8, Pallas kernels, settle(): pl.pallas_call(functools.partial(settle_kernel, plan), grid=(1,), out_sha...  19.6 us
    ppermute x1, waiting for transfers between devices, on_device(): far = lax.ppermute(far, 'vol', across)  8.22 us
    ppermute x4, waiting for transfers between devices, on_device(): outer = [(*o, lax.ppermute(o[0], 'rate', rate_back)) for o in outer]  7.09 us
    ppermute x1, starting transfers between devices, on_device(): inner = (*inner, lax.ppermute(inner[0], 'rate', rate_back))  4.75 us
    ppermute x1, starting transfers between devices, on_device(): far = lax.ppermute(far, 'vol', across)  3.91 us
    unnamed x12, local copies, waits for them, and re-layouts  3.34 us
    ppermute x4, waiting for transfers between devices, on_device(): onward.append((lax.ppermute(pieces[1], 'rate', rate_on), *pieces))  3.11 us
    pallas_call x4, Pallas kernels, smooth_outer(): pl.pallas_call(outer_kernel, grid=(1,), out_shape=outs, in_specs=[SMEM] +...  2.68 us
  transfers between devices with their start and end apart: 11, of which 8 were waited for; matrix products, arithmetic and copies ran while one was open for 3% of the time, Pallas kernels for 33%

profile of v4, /device:TPU:25, one launch (start us, length us, event | category | flops | bytes accessed | tf_op | source)
XLA Modules:
  0.0 59.4 jit_solution(1564380260256656451)
XLA Ops:
  0.0 1.2 %copy-done = f32[16,8,2048]{2,1,0:T(8,128)S(1)} copy-done((f32[16,8,2048]{2,1,0:T(8,128)S(1)}, f32[16,8,2048]{2,1,0:T(8,128)}, u32[]{:S(2)}) %copy-start) | copy-done | bytes 1048600
  1.2 0.5 smooth_inner.1
  1.7 4.8 %collective-permute-start = (f32[6,8,2048]{2,1,0:T(8,128)S(1)}, f32[6,8,2048]{2,1,0:T(8,128)S(1)}, u32[]{:S(2)}, u32[]{:S(2)}) collective-permute-start(f32[6,8,2048]{2,1,0:T(8,128)S(1)} %get-tuple-element.38.refs_1_), channel_id=1, source_target_pairs={{0,7},{1,0},{2,1},{3,2},{4,3},{5,4},{6,5},{7,6},{8,15},{9,8},{10,9... | collective-permute-start | bytes 1179656 | tf_op jit(solution)/shard_map/ppermute | solution.py:368
  6.5 0.7 %copy-done.5 = f32[8,16]{1,0:T(8,128)S(1)} copy-done((f32[8,16]{1,0:T(8,128)S(1)}, f32[8,16]{1,0:T(8,128)}, u32[]{:S(2)}) %copy-start.5) | copy-done | bytes 536
  7.1 0.1 copy.12
  7.3 0.1 constant_dynamic-slice_fusion
  7.4 1.0 %collective-permute-start.1 = (f32[6,8,2176]{2,1,0:T(8,128)S(1)}, f32[6,8,2176]{2,1,0:T(8,128)S(1)}, u32[]{:S(2)}, u32[]{:S(2)}) collective-permute-start(f32[6,8,2176]{2,1,0:T(8,128)S(1)} %pad_maximum_fusion), channel_id=1, source_target_pairs={{0,8},{8,0},{16,24},{24,16},{32,40},{40,32},{48,56},{56,48},{64,72... | collective-permute-start | bytes 1253384 | tf_op jit(solution)/shard_map/ppermute | solution.py:365
  8.4 0.8 %pad_maximum_fusion.1 = f32[6,8,2176]{2,1,0:T(8,128)} fusion(f32[6,8,128]{2,1,0:T(8,128)S(1)} %get-tuple-element.79, f32[6,8,2048]{2,1,0:T(8,128)S(1)} %get-tuple-element.73), kind=kLoop, calls=%fused_computation.1 | loop fusion | flops 104448 | bytes 835584 | tf_op jit(solution)/shard_map/concatenate | solution.py:361
  9.2 3.9 %collective-permute-start.2 = (f32[6,8,2176]{2,1,0:T(8,128)}, f32[6,8,2176]{2,1,0:T(8,128)S(1)}, u32[]{:S(2)}, u32[]{:S(2)}) collective-permute-start(f32[6,8,2176]{2,1,0:T(8,128)} %pad_maximum_fusion.1), channel_id=1, source_target_pairs={{8,16},{16,8},{24,32},{32,24},{40,48},{48,40},{56,64},{64,56},{72,... | collective-permute-start | bytes 1253384 | tf_op jit(solution)/shard_map/ppermute | solution.py:364
  13.2 0.1 stack.23
  13.4 0.8 %copy-done.4 = s32[8,2048]{1,0:T(8,128)S(1)} copy-done((s32[8,2048]{1,0:T(8,128)S(1)}, s32[8,2048]{1,0:T(8,128)}, u32[]{:S(2)}) %copy-start.4) | copy-done | bytes 65560
  14.2 0.0 collective-permute-done.1.near
  14.2 8.2 %collective-permute-done.2.far = f32[6,8,2176]{2,1,0:T(8,128)S(1)} collective-permute-done((f32[6,8,2176]{2,1,0:T(8,128)}, f32[6,8,2176]{2,1,0:T(8,128)S(1)}, u32[]{:S(2)}, u32[]{:S(2)}) %collective-permute-start.2) | collective-permute-done | bytes 417824 | tf_op jit(solution)/shard_map/ppermute | solution.py:364
  22.4 0.1 select_reduce_fusion.1
  22.5 0.1 copy.14
  22.6 0.1 copy.13
  22.7 0.7 %smooth_outer.7 = (f32[6,16,512]{2,1,0:T(8,128)S(1)}, f32[2,16,512]{2,1,0:T(8,128)S(1)}) custom-call(s32[5]{0:T(128)S(1)} %convert_element_type.17.side.refs_0_, f32[16,8,2048]{2,1,0:T(8,128)S(1)} %copy-done.1, f32[6,8,2176]{2,1,0:T(8,128)S(1)} %collective-permute-done.1.near, f32[6,8,2176]{2,1,0:T(8,128)S(1)} %collective-permute-done.2.far), custom_call_target="tpu_custom_call" | custom-call | flops 1000000000 | tf_op jit(solution)/shard_map/smooth_outer/pallas_call | solution.py:136
  23.4 0.3 collective-permute-start.6
  23.7 0.7 %smooth_outer.6 = (f32[6,16,512]{2,1,0:T(8,128)S(1)}, f32[2,16,512]{2,1,0:T(8,128)S(1)}) custom-call(s32[5]{0:T(128)S(1)} %convert_element_type.17.side.refs_0_, f32[16,8,2048]{2,1,0:T(8,128)S(1)} %copy-done.1, f32[6,8,2176]{2,1,0:T(8,128)S(1)} %collective-permute-done.1.near, f32[6,8,2176]{2,1,0:T(8,128)S(1)} %collective-permute-done.2.far), custom_call_target="tpu_custom_call" | custom-call | flops 1000000000 | tf_op jit(solution)/shard_map/smooth_outer/pallas_call | solution.py:136
  24.3 1.1 %collective-permute-start.5 = (f32[6,16,512]{2,1,0:T(8,128)S(1)}, f32[6,16,512]{2,1,0:T(8,128)S(1)}, u32[]{:S(2)}, u32[]{:S(2)}) collective-permute-start(f32[6,16,512]{2,1,0:T(8,128)S(1)} %get-tuple-element.44.refs_4_), channel_id=1, source_target_pairs={{0,7},{1,0},{2,1},{3,2},{4,3},{5,4},{6,5},{7,6},{8,15},{9,8},{10,9... | collective-permute-start | bytes 589832 | tf_op jit(solution)/shard_map/ppermute | solution.py:370
  25.5 0.7 %smooth_outer.5 = (f32[6,16,512]{2,1,0:T(8,128)S(1)}, f32[2,16,512]{2,1,0:T(8,128)S(1)}) custom-call(s32[5]{0:T(128)S(1)} %convert_element_type.17.side.refs_0_, f32[16,8,2048]{2,1,0:T(8,128)S(1)} %copy-done.1, f32[6,8,2176]{2,1,0:T(8,128)S(1)} %collective-permute-done.1.near, f32[6,8,2176]{2,1,0:T(8,128)S(1)} %collective-permute-done.2.far), custom_call_target="tpu_custom_call" | custom-call | flops 1000000000 | tf_op jit(solution)/shard_map/smooth_outer/pallas_call | solution.py:136
  26.2 0.3 collective-permute-start.4
  26.5 0.7 %smooth_outer.4 = (f32[6,16,512]{2,1,0:T(8,128)S(1)}, f32[2,16,512]{2,1,0:T(8,128)S(1)}) custom-call(s32[5]{0:T(128)S(1)} %convert_element_type.17.side.refs_0_, f32[16,8,2048]{2,1,0:T(8,128)S(1)} %copy-done.1, f32[6,8,2176]{2,1,0:T(8,128)S(1)} %collective-permute-done.1.near, f32[6,8,2176]{2,1,0:T(8,128)S(1)} %collective-permute-done.2.far), custom_call_target="tpu_custom_call" | custom-call | flops 1000000000 | tf_op jit(solution)/shard_map/smooth_outer/pallas_call | solution.py:136
  27.1 0.8 %collective-permute-start.3 = (f32[6,16,512]{2,1,0:T(8,128)S(1)}, f32[6,16,512]{2,1,0:T(8,128)S(1)}, u32[]{:S(2)}, u32[]{:S(2)}) collective-permute-start(f32[6,16,512]{2,1,0:T(8,128)S(1)} %get-tuple-element.40.refs_4_), channel_id=1, source_target_pairs={{0,7},{1,0},{2,1},{3,2},{4,3},{5,4},{6,5},{7,6},{8,15},{9,8},{10,9... | collective-permute-start | bytes 589832 | tf_op jit(solution)/shard_map/ppermute | solution.py:370
  28.0 0.1 fusion.5
  28.1 0.0 collective-permute-done.refs_3_
  28.1 2.3 %collective-permute-done.6.refs_6_ = f32[6,16,512]{2,1,0:T(8,128)S(1)} collective-permute-done((f32[6,16,512]{2,1,0:T(8,128)S(1)}, f32[6,16,512]{2,1,0:T(8,128)S(1)}, u32[]{:S(2)}, u32[]{:S(2)}) %collective-permute-start.6) | collective-permute-done | bytes 196640 | tf_op jit(solution)/shard_map/ppermute | solution.py:370
  30.4 0.1 broadcast_in_dim.9.refs_12_
  30.5 0.6 %copy-done.2 = f32[2048]{0:T(1024)S(1)} copy-done((f32[2048]{0:T(1024)S(1)}, f32[2048]{0:T(1024)}, u32[]{:S(2)}) %copy-start.2) | copy-done | bytes 8216
  31.1 2.1 %settle.8 = (f32[2,16,384]{2,1,0:T(8,128)S(1)}, f32[6,16,384]{2,1,0:T(8,128)S(1)}, bf16[384,128]{1,0:T(8,128)(2,1)S(1)}, f32[192,128]{1,0:T(8,128)S(1)}) custom-call(s32[5]{0:T(128)S(1)} %convert_element_type.17.side.refs_0_, f32[6,8,2048]{2,1,0:T(8,128)S(1)} %get-tuple-element.38.refs_1_, f32[2,8,2048]{2,1,0:T(8,128)S(1)} %get-tuple-element.39.refs_2_, ...), custom_call_target="tpu_custom_call" | custom-call | flops 4000000000 | tf_op jit(solution)/shard_map/settle/pallas_call | solution.py:325
  33.2 0.1 collective-permute-start.10
  33.3 1.3 %collective-permute-done.5.refs_6_ = f32[6,16,512]{2,1,0:T(8,128)S(1)} collective-permute-done((f32[6,16,512]{2,1,0:T(8,128)S(1)}, f32[6,16,512]{2,1,0:T(8,128)S(1)}, u32[]{:S(2)}, u32[]{:S(2)}) %collective-permute-start.5) | collective-permute-done | bytes 196640 | tf_op jit(solution)/shard_map/ppermute | solution.py:370
  34.6 2.4 %settle.9 = (f32[2,16,512]{2,1,0:T(8,128)S(1)}, f32[6,16,512]{2,1,0:T(8,128)S(1)}, bf16[384,128]{1,0:T(8,128)(2,1)S(1)}, f32[192,128]{1,0:T(8,128)S(1)}) custom-call(s32[5]{0:T(128)S(1)} %convert_element_type.17.side.refs_0_, f32[6,8,2048]{2,1,0:T(8,128)S(1)} %get-tuple-element.38.refs_1_, f32[2,8,2048]{2,1,0:T(8,128)S(1)} %get-tuple-element.39.refs_2_, ...), custom_call_target="tpu_custom_call" | custom-call | flops 4000000000 | tf_op jit(solution)/shard_map/settle/pallas_call | solution.py:325
  37.1 0.1 collective-permute-start.9
  37.2 1.7 %collective-permute-done.4.refs_6_ = f32[6,16,512]{2,1,0:T(8,128)S(1)} collective-permute-done((f32[6,16,512]{2,1,0:T(8,128)S(1)}, f32[6,16,512]{2,1,0:T(8,128)S(1)}, u32[]{:S(2)}, u32[]{:S(2)}) %collective-permute-start.4) | collective-permute-done | bytes 196640 | tf_op jit(solution)/shard_map/ppermute | solution.py:370
  38.8 2.4 %settle.10 = (f32[2,16,512]{2,1,0:T(8,128)S(1)}, f32[6,16,512]{2,1,0:T(8,128)S(1)}, bf16[384,128]{1,0:T(8,128)(2,1)S(1)}, f32[192,128]{1,0:T(8,128)S(1)}) custom-call(s32[5]{0:T(128)S(1)} %convert_element_type.17.side.refs_0_, f32[6,8,2048]{2,1,0:T(8,128)S(1)} %get-tuple-element.38.refs_1_, f32[2,8,2048]{2,1,0:T(8,128)S(1)} %get-tuple-element.39.refs_2_, ...), custom_call_target="tpu_custom_call" | custom-call | flops 4000000000 | tf_op jit(solution)/shard_map/settle/pallas_call | solution.py:325
  41.3 0.1 collective-permute-start.8
  41.4 1.7 %collective-permute-done.3.refs_6_ = f32[6,16,512]{2,1,0:T(8,128)S(1)} collective-permute-done((f32[6,16,512]{2,1,0:T(8,128)S(1)}, f32[6,16,512]{2,1,0:T(8,128)S(1)}, u32[]{:S(2)}, u32[]{:S(2)}) %collective-permute-start.3) | collective-permute-done | bytes 196640 | tf_op jit(solution)/shard_map/ppermute | solution.py:370
  43.1 2.8 %settle.11 = (f32[2,16,640]{2,1,0:T(8,128)S(1)}, f32[6,16,640]{2,1,0:T(8,128)S(1)}) custom-call(s32[5]{0:T(128)S(1)} %convert_element_type.17.side.refs_0_, f32[6,8,2048]{2,1,0:T(8,128)S(1)} %get-tuple-element.38.refs_1_, f32[2,8,2048]{2,1,0:T(8,128)S(1)} %get-tuple-element.39.refs_2_, f32[6,8,2048]{2,1,0:T(8,128)S(1)} %collective-permute-done.refs_3_, ...), custom_call_target="tpu_custom_call" | custom-call | flops 4000000000 | tf_op jit(solution)/shard_map/settle/pallas_call | solution.py:325
  45.9 0.3 collective-permute-start.7
  46.1 0.1 broadcast_in_dim.21.refs_9_
  46.2 2.0 %settle.12 = (f32[16,8,2048]{2,1,0:T(8,128)}, bf16[256,128]{1,0:T(8,128)(2,1)S(1)}, f32[128,128]{1,0:T(8,128)S(1)}) custom-call(s32[5]{0:T(128)S(1)} %convert_element_type.17.side.refs_0_, f32[6,16,384]{2,1,0:T(8,128)S(1)} %collective-permute-done.10.refs_1_, f32[2,16,384]{2,1,0:T(8,128)S(1)} %get-tuple-element.61.refs_2_, ...), custom_call_target="tpu_custom_call" | custom-call | flops 4000000000 | tf_op jit(solution)/shard_map/settle/pallas_call | solution.py:325
  48.2 2.1 %collective-permute-done.9.refs_1_ = f32[6,16,512]{2,1,0:T(8,128)S(1)} collective-permute-done((f32[6,16,512]{2,1,0:T(8,128)S(1)}, f32[6,16,512]{2,1,0:T(8,128)S(1)}, u32[]{:S(2)}, u32[]{:S(2)}) %collective-permute-start.9) | collective-permute-done | bytes 196640 | tf_op jit(solution)/shard_map/ppermute | solution.py:388
  50.3 2.5 %settle.13 = (f32[16,8,2048]{2,1,0:T(8,128)}, bf16[256,128]{1,0:T(8,128)(2,1)S(1)}, f32[128,128]{1,0:T(8,128)S(1)}) custom-call(s32[5]{0:T(128)S(1)} %convert_element_type.17.side.refs_0_, f32[6,16,512]{2,1,0:T(8,128)S(1)} %collective-permute-done.9.refs_1_, f32[2,16,512]{2,1,0:T(8,128)S(1)} %get-tuple-element.59.refs_2_, ...), custom_call_target="tpu_custom_call", output_to_operand_aliasing={{0}: (13, {})} | custom-call | flops 4000000000 | tf_op jit(solution)/shard_map/settle/pallas_call | solution.py:325
  52.8 0.9 %collective-permute-done.8.refs_1_ = f32[6,16,512]{2,1,0:T(8,128)S(1)} collective-permute-done((f32[6,16,512]{2,1,0:T(8,128)S(1)}, f32[6,16,512]{2,1,0:T(8,128)S(1)}, u32[]{:S(2)}, u32[]{:S(2)}) %collective-permute-start.8) | collective-permute-done | bytes 196640 | tf_op jit(solution)/shard_map/ppermute | solution.py:388
  53.6 2.5 %settle.14 = (f32[16,8,2048]{2,1,0:T(8,128)}, bf16[256,128]{1,0:T(8,128)(2,1)S(1)}, f32[128,128]{1,0:T(8,128)S(1)}) custom-call(s32[5]{0:T(128)S(1)} %convert_element_type.17.side.refs_0_, f32[6,16,512]{2,1,0:T(8,128)S(1)} %collective-permute-done.8.refs_1_, f32[2,16,512]{2,1,0:T(8,128)S(1)} %get-tuple-element.57.refs_2_, ...), custom_call_target="tpu_custom_call", output_to_operand_aliasing={{0}: (13, {})} | custom-call | flops 4000000000 | tf_op jit(solution)/shard_map/settle/pallas_call | solution.py:325
  56.1 0.2 collective-permute-done.7.refs_1_
  56.2 3.0 %settle.15 = f32[16,8,2048]{2,1,0:T(8,128)} custom-call(s32[5]{0:T(128)S(1)} %convert_element_type.17.side.refs_0_, f32[6,16,640]{2,1,0:T(8,128)S(1)} %collective-permute-done.7.refs_1_, f32[2,16,640]{2,1,0:T(8,128)S(1)} %get-tuple-element.55.refs_2_, f32[6,16,640]{2,1,0:T(8,128)S(1)} %get-tuple-element.54.refs_3_, ...), custom_call_target="tpu_custom_call", output_to_operand_aliasing={{}: (13, {})} | custom-call | flops 4000000000 | tf_op jit(solution)/shard_map/settle/pallas_call | solution.py:325
  (19 shorter events, 0.1 us)
Async XLA Ops:
  0.0 1.2 %copy-start = (f32[16,8,2048]{2,1,0:T(8,128)S(1)}, f32[16,8,2048]{2,1,0:T(8,128)}, u32[]{:S(2)}) copy-start(f32[16,8,2048]{2,1,0:T(8,128)} %own.9) | copy-start | bytes 3145732
  1.2 6.1 %copy-start.1 = (f32[16,8,2048]{2,1,0:T(8,128)S(1)}, f32[16,8,2048]{2,1,0:T(8,128)}, u32[]{:S(2)}) copy-start(f32[16,8,2048]{2,1,0:T(8,128)} %own.9) | copy-start | bytes 3145732
  1.7 26.4 %collective-permute-start = (f32[6,8,2048]{2,1,0:T(8,128)S(1)}, f32[6,8,2048]{2,1,0:T(8,128)S(1)}, u32[]{:S(2)}, u32[]{:S(2)}) collective-permute-start(f32[6,8,2048]{2,1,0:T(8,128)S(1)} %get-tuple-element.38.refs_1_), channel_id=1, source_target_pairs={{0,7},{1,0},{2,1},{3,2},{4,3},{5,4},{6,5},{7,6},{8,15},{9,8},{10,9... | collective-permute-start | bytes 1179656 | tf_op jit(solution)/shard_map/ppermute | solution.py:368
  6.5 0.7 %copy-start.5 = (f32[8,16]{1,0:T(8,128)S(1)}, f32[8,16]{1,0:T(8,128)}, u32[]{:S(2)}) copy-start(f32[8,16]{1,0:T(8,128)} %param.6) | copy-start | bytes 1540
  7.4 6.8 %collective-permute-start.1 = (f32[6,8,2176]{2,1,0:T(8,128)S(1)}, f32[6,8,2176]{2,1,0:T(8,128)S(1)}, u32[]{:S(2)}, u32[]{:S(2)}) collective-permute-start(f32[6,8,2176]{2,1,0:T(8,128)S(1)} %pad_maximum_fusion), channel_id=1, source_target_pairs={{0,8},{8,0},{16,24},{24,16},{32,40},{40,32},{48,56},{56,48},{64,72... | collective-permute-start | bytes 1253384 | tf_op jit(solution)/shard_map/ppermute | solution.py:365
  8.4 4.9 %copy-start.3 = (f32[8,2048]{1,0:T(8,128)S(1)}, f32[8,2048]{1,0:T(8,128)}, u32[]{:S(2)}) copy-start(f32[8,2048]{1,0:T(8,128)} %param.8) | copy-start | bytes 196612
  9.2 13.2 %collective-permute-start.2 = (f32[6,8,2176]{2,1,0:T(8,128)}, f32[6,8,2176]{2,1,0:T(8,128)S(1)}, u32[]{:S(2)}, u32[]{:S(2)}) collective-permute-start(f32[6,8,2176]{2,1,0:T(8,128)} %pad_maximum_fusion.1), channel_id=1, source_target_pairs={{8,16},{16,8},{24,32},{32,24},{40,48},{48,40},{56,64},{64,56},{72,... | collective-permute-start | bytes 1253384 | tf_op jit(solution)/shard_map/ppermute | solution.py:364
  13.3 0.8 %copy-start.4 = (s32[8,2048]{1,0:T(8,128)S(1)}, s32[8,2048]{1,0:T(8,128)}, u32[]{:S(2)}) copy-start(s32[8,2048]{1,0:T(8,128)} %param.7) | copy-start | bytes 196612
  23.4 7.1 %collective-permute-start.6 = (f32[6,16,512]{2,1,0:T(8,128)S(1)}, f32[6,16,512]{2,1,0:T(8,128)S(1)}, u32[]{:S(2)}, u32[]{:S(2)}) collective-permute-start(f32[6,16,512]{2,1,0:T(8,128)S(1)} %get-tuple-element.46.refs_4_), channel_id=1, source_target_pairs={{0,7},{1,0},{2,1},{3,2},{4,3},{5,4},{6,5},{7,6},{8,15},{9,8},{10,9... | collective-permute-start | bytes 589832 | tf_op jit(solution)/shard_map/ppermute | solution.py:370
  24.3 10.3 %collective-permute-start.5 = (f32[6,16,512]{2,1,0:T(8,128)S(1)}, f32[6,16,512]{2,1,0:T(8,128)S(1)}, u32[]{:S(2)}, u32[]{:S(2)}) collective-permute-start(f32[6,16,512]{2,1,0:T(8,128)S(1)} %get-tuple-element.44.refs_4_), channel_id=1, source_target_pairs={{0,7},{1,0},{2,1},{3,2},{4,3},{5,4},{6,5},{7,6},{8,15},{9,8},{10,9... | collective-permute-start | bytes 589832 | tf_op jit(solution)/shard_map/ppermute | solution.py:370
  26.2 12.7 %collective-permute-start.4 = (f32[6,16,512]{2,1,0:T(8,128)S(1)}, f32[6,16,512]{2,1,0:T(8,128)S(1)}, u32[]{:S(2)}, u32[]{:S(2)}) collective-permute-start(f32[6,16,512]{2,1,0:T(8,128)S(1)} %get-tuple-element.42.refs_4_), channel_id=1, source_target_pairs={{0,7},{1,0},{2,1},{3,2},{4,3},{5,4},{6,5},{7,6},{8,15},{9,8},{10,9... | collective-permute-start | bytes 589832 | tf_op jit(solution)/shard_map/ppermute | solution.py:370
  27.1 15.9 %collective-permute-start.3 = (f32[6,16,512]{2,1,0:T(8,128)S(1)}, f32[6,16,512]{2,1,0:T(8,128)S(1)}, u32[]{:S(2)}, u32[]{:S(2)}) collective-permute-start(f32[6,16,512]{2,1,0:T(8,128)S(1)} %get-tuple-element.40.refs_4_), channel_id=1, source_target_pairs={{0,7},{1,0},{2,1},{3,2},{4,3},{5,4},{6,5},{7,6},{8,15},{9,8},{10,9... | collective-permute-start | bytes 589832 | tf_op jit(solution)/shard_map/ppermute | solution.py:370
  30.4 0.7 %copy-start.2 = (f32[2048]{0:T(1024)S(1)}, f32[2048]{0:T(1024)}, u32[]{:S(2)}) copy-start(f32[2048]{0:T(1024)} %param.9) | copy-start | bytes 24580
  33.2 12.9 %collective-permute-start.10 = (f32[6,16,384]{2,1,0:T(8,128)S(1)}, f32[6,16,384]{2,1,0:T(8,128)S(1)}, u32[]{:S(2)}, u32[]{:S(2)}) collective-permute-start(f32[6,16,384]{2,1,0:T(8,128)S(1)} %get-tuple-element.60.refs_3_), channel_id=1, source_target_pairs={{0,1},{1,2},{2,3},{3,4},{4,5},{5,6},{6,7},{7,0},{8,9},{9,10},{10,1... | collective-permute-start | bytes 442376 | tf_op jit(solution)/shard_map/ppermute | solution.py:388
  37.1 13.2 %collective-permute-start.9 = (f32[6,16,512]{2,1,0:T(8,128)S(1)}, f32[6,16,512]{2,1,0:T(8,128)S(1)}, u32[]{:S(2)}, u32[]{:S(2)}) collective-permute-start(f32[6,16,512]{2,1,0:T(8,128)S(1)} %get-tuple-element.58.refs_3_), channel_id=1, source_target_pairs={{0,1},{1,2},{2,3},{3,4},{4,5},{5,6},{6,7},{7,0},{8,9},{9,10},{10,1... | collective-permute-start | bytes 589832 | tf_op jit(solution)/shard_map/ppermute | solution.py:388
  41.3 12.3 %collective-permute-start.8 = (f32[6,16,512]{2,1,0:T(8,128)S(1)}, f32[6,16,512]{2,1,0:T(8,128)S(1)}, u32[]{:S(2)}, u32[]{:S(2)}) collective-permute-start(f32[6,16,512]{2,1,0:T(8,128)S(1)} %get-tuple-element.56.refs_3_), channel_id=1, source_target_pairs={{0,1},{1,2},{2,3},{3,4},{4,5},{5,6},{6,7},{7,0},{8,9},{9,10},{10,1... | collective-permute-start | bytes 589832 | tf_op jit(solution)/shard_map/ppermute | solution.py:388
  45.9 10.4 %collective-permute-start.7 = (f32[6,16,640]{2,1,0:T(8,128)S(1)}, f32[6,16,640]{2,1,0:T(8,128)S(1)}, u32[]{:S(2)}, u32[]{:S(2)}) collective-permute-start(f32[6,16,640]{2,1,0:T(8,128)S(1)} %get-tuple-element.54.refs_3_), channel_id=1, source_target_pairs={{0,1},{1,2},{2,3},{3,4},{4,5},{5,6},{6,7},{7,0},{8,9},{9,10},{10,1... | collective-permute-start | bytes 737288 | tf_op jit(solution)/shard_map/ppermute | solution.py:388
